TPU v7x, 128 devices: a whole 4x4x4 slice. The times are simulated.
128 devices in a mesh: dp: 16 (over z, y), tensor: 8 (over x, core).
Axes of the slice: x: 4, y: 4, z: 4, core: 2. Of those that a mesh axis runs over, the one named last changes fastest.
Arguments:
- acts: bfloat16 [24576, 6144], P('dp', 'tensor'), may hold values from -600 to 600, as said below
- grads_out: bfloat16 [24576, 24576], P('dp', 'tensor'), may hold values from -600 to 600, as said below
- sketch_in: bfloat16 [6144, 256], P('tensor'), may hold values from -0.078125 to 0.078125
- sketch_out: bfloat16 [24576, 256], P('tensor'), may hold values from -0.0390625 to 0.0390625
- weight_grad: float32 [6144, 24576], P('dp', 'tensor'), may hold values from -6 to 6
Outputs:
- precond: float32 [6144, 24576], P('dp', 'tensor')
Inputs may be any that keep to these rules, and one draw needn't show every extreme that they name: acts: rows and columns of varying scale. grads_out: rows and columns of varying scale.
All inputs are finite; a program needn't handle non-finite values.
Results may differ from a plain program's by a relative error of at most 0.0015.
Values sent between devices are 32-bit elements; how exact they have to be, the bound alone decides.
No kernel may reach another device: no remote copies, remote signals or barrier semaphores. Data moves between devices by JAX's collectives and lax.ppermute only.
A program may use at most 128 MiB of HBM per device.

v0:
```python
import functools

import jax
import jax.numpy as jnp
from jax import lax
from jax.experimental import pallas as pl
from jax.experimental.pallas import tpu as pltpu
from jax.sharding import PartitionSpec as P

D = 6144
FF = 24576
R = 256
TILE = 512
BLOCK = 64
VMEM_LIMIT = 60 * 1024 * 1024

DAMPING = 0.1


def ring(kind, step):
    if kind == "y":
        return [(i, i // 4 * 4 + (i % 4 + step) % 4) for i in range(16)]
    if kind == "z":
        return [(i, (i // 4 + step) % 4 * 4 + i % 4) for i in range(16)]
    return [(i, (i // 2 + step) % 4 * 2 + i % 2) for i in range(8)]


def send(value, kind, step):
    return lax.ppermute(value, "tensor" if kind == "x" else "dp", ring(kind, step))


def swap_cores(value):
    return lax.ppermute(value, "tensor", [(i, i ^ 1) for i in range(8)])


def place(kind):
    if kind == "y":
        return lax.axis_index("dp") % 4
    if kind == "z":
        return lax.axis_index("dp") // 4
    return lax.axis_index("tensor") // 2


def rows(value, index, count):
    return lax.dynamic_slice_in_dim(value, index * count, count, 0)


def scatter_four(value, kind):
    here, count = place(kind), value.shape[0] // 4
    two, one, three = (
        send(rows(value, (here + step) % 4, count), kind, step) for step in (2, 1, 3)
    )
    return (rows(value, here, count) + two) + (one + three)


def gather_four(value, kind):
    here, count = place(kind), value.shape[0]
    two, one, three = (send(value, kind, step) for step in (2, 1, 3))
    whole = jnp.zeros((4 * count,) + value.shape[1:], value.dtype)
    for step, part in enumerate((value, one, two, three)):
        whole = lax.dynamic_update_slice_in_dim(whole, part, (here - step) % 4 * count, 0)
    return whole


def scatter_dp(first, second):
    first, second = scatter_four(first, "y"), scatter_four(second, "z")
    return jnp.concatenate([scatter_four(first, "z"), scatter_four(second, "y")])


def scatter_dp_after(first, second, after):
    halves = []
    for value, kind in ((first, "y"), (second, "z")):
        here, count = place(kind), value.shape[0] // 4
        parts = [
            send(rows(value, (here + step) % 4, count), kind, step) for step in (2, 1, 3)
        ]
        halves.append(sum_blocks(here, value, parts, after))
    return jnp.concatenate([scatter_four(halves[0], "z"), scatter_four(halves[1], "y")])


def sum_kernel(here, value, two, one, three, after, out):
    out[...] = (value[...] + two[...]) + (one[...] + three[...])


def sum_blocks(here, value, parts, after):
    count, columns = parts[0].shape
    whole = pl.BlockSpec((count, columns), lambda i, h: (0, 0))
    grid_spec = pltpu.PrefetchScalarGridSpec(
        num_scalar_prefetch=1,
        grid=(1,),
        in_specs=[pl.BlockSpec((count, columns), lambda i, h: (h[0], 0))]
        + [whole] * 3
        + [pl.BlockSpec(memory_space=pl.ANY)],
        out_specs=whole,
    )
    return call(sum_kernel, array(count, columns), grid_spec=grid_spec, name="sum_blocks")(
        here.astype(jnp.int32).reshape(1), value, *parts, after
    )


def store_groups(first, second, columns, value):
    for d in range(16):
        to = d % 4 * 4 + d // 4
        first[8 * to : 8 * to + 8, columns] = value[16 * d : 16 * d + 8]
        second[8 * d : 8 * d + 8, columns] = value[16 * d + 8 : 16 * d + 16]


def tensor_chunk():
    index = lax.axis_index("tensor")
    return index % 2 * 4 + index // 2


def scatter_tensor(value):
    core, half = lax.axis_index("tensor") % 2, value.shape[0] // 2
    other = swap_cores(rows(value, 1 - core, half))
    return scatter_four(rows(value, core, half) + other, "x")


def gather_tensor(value):
    core = lax.axis_index("tensor") % 2
    value = gather_four(value, "x")
    other = swap_cores(value)
    low = jnp.where(core == 0, value, other)
    high = jnp.where(core == 0, other, value)
    return jnp.concatenate([low, high])


def split(value):
    high = value.astype(jnp.bfloat16)
    return high, (value - high.astype(jnp.float32)).astype(jnp.bfloat16)


def product(left, right, dims):
    (lh, ll), (rh, rl) = left, right
    (along_left,), (along_right,) = dims
    return lax.dot_general(
        jnp.concatenate([lh, lh, ll], axis=along_left),
        jnp.concatenate([rh, rl, rh], axis=along_right),
        (dims, ((), ())),
        preferred_element_type=jnp.float32,
    )


def call(kernel, out_shape, **options):
    return pl.pallas_call(
        kernel,
        out_shape=out_shape,
        compiler_params=pltpu.CompilerParams(vmem_limit_bytes=VMEM_LIMIT),
        **options,
    )


def array(*shape):
    return jax.ShapeDtypeStruct(shape, jnp.float32)


def sketch_kernel(core, grads, acts, sketch_out, sketch_in, out, squares, total_grad, total_act):
    step = pl.program_id(0)
    some = zip((grads, acts), (sketch_out, sketch_in), (total_grad, total_act))
    for i, (value, sketch, total) in enumerate(some):

        @pl.when(step == 0)
        def _():
            total[...] = jnp.zeros_like(total)

        tile = value[...]
        out[:, i * R : i * R + R] = jnp.dot(
            tile, sketch[...], preferred_element_type=jnp.float32
        )
        tile = tile.astype(jnp.float32)
        total[...] += jnp.sum(jnp.square(tile).reshape(-1, 8, tile.shape[1]), axis=0)

        @pl.when(step == pl.num_programs(0) - 1)
        def _():
            whole = jnp.sum(total[...], keepdims=True)
            squares[8 * i : 8 * i + 8, :] = jnp.broadcast_to(whole, (8, 128))


def sketches(half, grads, acts, sketch_out, sketch_in):
    count = grads.shape[0] // 2
    step = 384
    steps = count // step
    tile = lambda columns: pl.BlockSpec((step, columns), lambda i, h: (h[0] * steps + i, 0))
    whole = lambda value: pl.BlockSpec(value.shape, lambda i, h: (0, 0))
    grid_spec = pltpu.PrefetchScalarGridSpec(
        num_scalar_prefetch=1,
        grid=(steps,),
        in_specs=[
            tile(grads.shape[1]),
            tile(acts.shape[1]),
            whole(sketch_out),
            whole(sketch_in),
        ],
        out_specs=[
            pl.BlockSpec((step, 2 * R), lambda i, h: (i, 0)),
            pl.BlockSpec((16, 128), lambda i, h: (0, 0)),
        ],
        scratch_shapes=[
            pltpu.VMEM((8, grads.shape[1]), jnp.float32),
            pltpu.VMEM((8, acts.shape[1]), jnp.float32),
        ],
    )
    return call(
        sketch_kernel,
        [array(count, 2 * R), array(16, 128)],
        grid_spec=grid_spec,
        name="sketches",
    )(half.astype(jnp.int32).reshape(1), grads, acts, sketch_out, sketch_in)


LAST = ((1,), (1,))
INNER = ((1,), (0,))


def flip_halves(core, own, other, flipped):
    half = own.shape[0]
    flipped[:, pl.ds(pl.multiple_of(core * half, 128), half)] = own[...].T
    flipped[:, pl.ds(pl.multiple_of((1 - core) * half, 128), half)] = other[...].T


def range_grad_kernel(
    tokens_all, place_ref, own, other, grads, sq_one, sq_two, act, first, second, piece, flipped, rounded
):
    step = pl.program_id(0)
    columns = grads.shape[1]

    @pl.when(step == 0)
    def _():
        flip_halves(place_ref[1], own, other, flipped)
        rounded[...] = flipped[...].astype(jnp.bfloat16)
        total = act[0:48, :]
        for d in range(1, 16):
            total += act[48 * d : 48 * d + 48, :]
        piece[...] = total

    part = jnp.dot(rounded[...], grads[...], preferred_element_type=jnp.float32)
    to = pl.ds(pl.multiple_of(step * columns, 128), columns)
    store_groups(first, second, to, part / tokens_all)

    @pl.when(step == pl.num_programs(0) - 1)
    def _():
        some = flipped[pl.ds(pl.multiple_of(place_ref[0] * 32, 32), 32), :]
        core = product(split(flipped[...]), split(some), LAST) / tokens_all
        lane = lax.broadcasted_iota(jnp.int32, (R, 96), 1)
        squares = sq_one[...] + sq_two[...]
        traces = jnp.where(lane == 0, squares[0:1, 0:1], 0.0)
        traces = jnp.where(lane == 1, squares[8:9, 0:1], traces)
        rest = jnp.concatenate([core, traces], axis=1)
        store_groups(first, second, pl.ds(first.shape[1] - 128, 128), rest)


def range_grad_of(places, own, other, grads, sq_one, sq_two, act, tokens_all):
    count, columns = grads.shape
    whole = lambda shape: pl.BlockSpec(shape, lambda j, c: (0, 0))
    grid_spec = pltpu.PrefetchScalarGridSpec(
        num_scalar_prefetch=1,
        grid=(columns // TILE,),
        in_specs=[
            whole((count // 2, R)),
            whole((count // 2, R)),
            pl.BlockSpec((count, TILE), lambda j, c: (0, j)),
            whole((16, 128)),
            whole((16, 128)),
            whole((768, R)),
        ],
        out_specs=[whole((R // 2, columns + 128))] * 2 + [whole((48, R))],
        scratch_shapes=[
            pltpu.VMEM((R, count), jnp.float32),
            pltpu.VMEM((R, count), jnp.bfloat16),
        ],
    )
    return call(
        functools.partial(range_grad_kernel, tokens_all),
        [array(R // 2, columns + 128)] * 2 + [array(48, R)],
        grid_spec=grid_spec,
        name="range_grad",
    )(places, own, other, grads, sq_one, sq_two, act)


def range_act_kernel(tokens_all, place_ref, own, other, acts, out, core, flipped):
    flip_halves(place_ref[1], own, other, flipped)
    part = jnp.dot(
        flipped[...].astype(jnp.bfloat16), acts[...], preferred_element_type=jnp.float32
    )
    out[...] = part.T / tokens_all
    some = flipped[pl.ds(pl.multiple_of(place_ref[0] * 32, 32), 32), :]
    core[:, :32] = product(split(flipped[...]), split(some), LAST) / tokens_all
    core[:, 32:] = jnp.zeros((R, 96), jnp.float32)


def range_act_of(places, own, other, acts, tokens_all):
    count, columns = acts.shape
    whole = lambda shape, j=0: pl.BlockSpec(shape, lambda i, c: (0, j))
    grid_spec = pltpu.PrefetchScalarGridSpec(
        num_scalar_prefetch=1,
        grid=(1,),
        in_specs=[whole((count // 2, R), 1), whole((count // 2, R), 1), whole((count, columns))],
        out_specs=[whole((columns, R)), whole((R, 128))],
        scratch_shapes=[pltpu.VMEM((R, count), jnp.float32)],
    )
    return call(
        functools.partial(range_act_kernel, tokens_all),
        [array(columns, R), array(R, 128)],
        grid_spec=grid_spec,
        name="range_act",
    )(places, own, other, acts)


def left_kernel(place_ref, rows_act, core, weight, first, second, flipped, high, low):
    step = pl.program_id(0)
    columns = weight.shape[1]

    @pl.when(step == 0)
    def _():
        flipped[...] = rows_act[...].T
        high[...], low[...] = split(flipped[...])
        some = flipped[pl.ds(pl.multiple_of(place_ref[0] * 32, 32), 32), :]
        gram = product((high[...], low[...]), split(some), LAST)
        rest = jnp.concatenate([gram, core[:, :96]], axis=1)
        store_groups(first, second, pl.ds(first.shape[1] - 128, 128), rest)

    part = product((high[...], low[...]), split(weight[...]), INNER)
    store_groups(first, second, pl.ds(pl.multiple_of(step * columns, 128), columns), part)


def left_products(places, rows_act, core, weight):
    count, columns = weight.shape
    whole = lambda shape: pl.BlockSpec(shape, lambda j, c: (0, 0))
    grid_spec = pltpu.PrefetchScalarGridSpec(
        num_scalar_prefetch=1,
        grid=(columns // TILE,),
        in_specs=[
            whole((count, R)),
            whole((R, 128)),
            pl.BlockSpec((count, TILE), lambda j, c: (0, j)),
        ],
        out_specs=[whole((R // 2, columns + 128))] * 2,
        scratch_shapes=[
            pltpu.VMEM((R, count), jnp.float32),
            pltpu.VMEM((R, count), jnp.bfloat16),
            pltpu.VMEM((R, count), jnp.bfloat16),
        ],
    )
    return call(
        left_kernel,
        [array(R // 2, columns + 128)] * 2,
        grid_spec=grid_spec,
        name="left_products",
    )(places, rows_act, core, weight)


def right_kernel(whole, weight, left, sums):
    @pl.when(pl.program_id(0) == 0)
    def _():
        sums[...] = jnp.zeros_like(sums)

    ranges = split(whole[...])
    right = product(split(weight[...]), ranges, LAST)
    gram = product(ranges, ranges, LAST)
    both = product(split(left[...]), ranges, LAST)
    for i in range(8):
        at = i * 88
        sums[at : at + 48, :] += right[i * 48 : i * 48 + 48]
        sums[at + 48 : at + 80, :] += gram[i * 32 : i * 32 + 32]
        sums[at + 80 : at + 82, :] += both[i * 2 : i * 2 + 2]


def right_products(whole, weight, left):
    count, columns = weight.shape
    return call(
        right_kernel,
        array(704, R),
        grid=(columns // TILE,),
        in_specs=[
            pl.BlockSpec((R, TILE), lambda j: (0, j)),
            pl.BlockSpec((count, TILE), lambda j: (0, j)),
            pl.BlockSpec((16, TILE), lambda j: (0, j)),
        ],
        out_specs=pl.BlockSpec((704, R), lambda j: (0, 0)),
        name="right_products",
    )(whole, weight, left)


def pack_small_kernel(parts, out):
    parts = [parts[i * 16 : i * 16 + 16, :] for i in range(8)]
    gram = jnp.concatenate([p[:, :32] for p in parts], axis=1)
    core = jnp.concatenate([p[:, 32:64] for p in parts], axis=1)
    for d in range(16):
        out[32 * d : 32 * d + 16, :] = gram
        out[32 * d + 16 : 32 * d + 32, :] = core


def pack_both_kernel(right, out):
    for d in range(16):
        for i in range(8):
            at = 16 * d + 2 * i
            out[at : at + 2, :] = right[i * 128 + 80 : i * 128 + 82, :]


def pack(kernel, value, count, name):
    whole = pl.BlockSpec(memory_space=pltpu.VMEM)
    return call(kernel, array(count, R), in_specs=[whole], out_specs=whole, name=name)(value)


def exact(left, right, dims):
    return lax.dot_general(
        left,
        right,
        (dims, ((), ())),
        precision=lax.Precision.HIGHEST,
        preferred_element_type=jnp.float32,
    )


def spread(value):
    return jnp.broadcast_to(value, (8, 2 * BLOCK))


def eliminate(matrices):
    sub = lax.broadcasted_iota(jnp.int32, (8, 2 * BLOCK), 0)
    count = BLOCK // 8
    groups = [[m[8 * i : 8 * i + 8] for i in range(count)] for m in matrices]
    for at in range(count):
        k = 8 * at
        for group in groups:
            tile = group[at]
            lines = [spread(tile[j : j + 1]) for j in range(8)]
            pivot = {
                (j, l): spread(lines[j][:, k + l : k + l + 1])
                for j in range(8)
                for l in range(j, 8)
            }
            scaled, factor = [], {}
            for j in range(8):
                inverse = 1.0 / pivot[j, j]
                scaled.append(lines[j] * inverse)
                for l in range(j + 1, 8):
                    factor[j, l] = pivot[j, l] * inverse
                    for m in range(l, 8):
                        pivot[l, m] = pivot[l, m] - factor[j, l] * pivot[j, m]
                    lines[l] = lines[l] - factor[j, l] * lines[j]
            for i in range(at + 1, count):
                value, sums, columns = group[i], None, []
                for j in range(8):
                    column = spread(value[:, k + j : k + j + 1])
                    for q in range(j):
                        column = column - columns[q] * factor[q, j]
                    columns.append(column)
                    term = column * scaled[j]
                    sums = term if sums is None else sums + term
                group[i] = value - sums
            for j in range(8):
                tile = jnp.where(sub == j, lines[j] * lax.rsqrt(pivot[j, j]), tile)
            group[at] = tile
    return [jnp.concatenate(group, axis=0) for group in groups]


def lower_inverses(work, outs):
    row = lax.broadcasted_iota(jnp.int32, (BLOCK, BLOCK), 0)
    column = lax.broadcasted_iota(jnp.int32, (BLOCK, BLOCK), 1)
    identity = jnp.where(row == column, 1.0, 0.0)
    for low in range(0, R, BLOCK):
        high = low + BLOCK
        done = eliminate(
            [jnp.concatenate([w[low:high, low:high], identity], axis=1) for w in work]
        )
        for w, corner, out in zip(work, done, outs):
            corner = jnp.where(row >= column, corner[:, BLOCK:], 0.0)
            line = exact(corner, w[low:high, :], INNER)
            out[low:high, :] = line[:, R:]
            if high < R:
                w[high:, :] -= exact(line[:, high:R], line, ((0,), (0,)))


def factor_kernel(counts, right, small, inverse_act, inverse_grad, scale, *work):
    trace_grad, trace_act = jnp.zeros((1, 1)), jnp.zeros((1, 1))
    for i in range(8):
        at = i * 128 + 120
        trace_grad += right[at : at + 1, 32:33]
        trace_act += right[at : at + 1, 33:34]
    damp_grad = DAMPING * trace_grad / counts[0]
    damp_act = DAMPING * trace_act / counts[1]
    scale[...] = jnp.broadcast_to(1.0 / (damp_act * damp_grad), (8, 128))
    row = lax.broadcasted_iota(jnp.int32, (R, R), 0)
    column = lax.broadcasted_iota(jnp.int32, (R, R), 1)
    identity = jnp.where(row == column, 1.0, 0.0)
    for w in work:
        w[:, R:] = identity
    for i in range(8):
        at, here = slice(i * 32, i * 32 + 32), i * 128
        work[1][at, :R] = damp_grad * right[here + 88 : here + 120, :] + right[here + 48 : here + 80, :]
    for d in range(16):
        at, here = slice(d * 16, d * 16 + 16), d * 32
        work[0][at, :R] = damp_act * small[here + 16 : here + 32, :] + small[here : here + 16, :]
    lower_inverses(work, (inverse_act, inverse_grad))


def factors(right, small, counts):
    whole = pl.BlockSpec(memory_space=pltpu.VMEM)
    return call(
        functools.partial(factor_kernel, counts),
        [array(R, R), array(R, R), array(8, 128)],
        in_specs=[whole] * 2,
        out_specs=[whole] * 3,
        scratch_shapes=[pltpu.VMEM((R, 2 * R), jnp.float32)] * 2,
        name="factors",
    )(right, small)


def applied(value, inverse):
    pieces = split(inverse)
    value = product(split(value), pieces, LAST)
    return product(split(value), pieces, INNER)


def last_kernel(
    left_sums, weight, range_grad, right, both, rows_act, inverse_act, inverse_grad, scale, out, sums, *pieces
):
    @pl.when(pl.program_id(0) == 0)
    def _():
        for i in range(8):
            sums[i * 48 : i * 48 + 48, :] = right[i * 128 : i * 128 + 48, :]
        solved = applied(rows_act[...], inverse_act[...])
        pieces[0][...], pieces[1][...] = split(solved)
        rest = sums[...] - product(split(solved), split(both[...]), INNER)
        pieces[2][...], pieces[3][...] = split(applied(rest, inverse_grad[...]))

    left = product((pieces[0][...], pieces[1][...]), split(left_sums[...]), INNER)
    range_pieces = split(range_grad[...])
    update = left + product((pieces[2][...], pieces[3][...]), range_pieces, INNER)
    out[...] = (weight[...] - update) * scale[0:1, 0:1]


def last_update(left_sums, weight, range_grad, *rest):
    count, columns = weight.shape
    return call(
        last_kernel,
        array(count, columns),
        grid=(columns // TILE,),
        in_specs=[
            pl.BlockSpec((R, TILE), lambda j: (0, j)),
            pl.BlockSpec((count, TILE), lambda j: (0, j)),
            pl.BlockSpec((R, TILE), lambda j: (0, j)),
        ]
        + [pl.BlockSpec(value.shape, lambda j: (0, 0)) for value in rest],
        out_specs=pl.BlockSpec((count, TILE), lambda j: (0, j)),
        scratch_shapes=[pltpu.VMEM((count, R), jnp.float32)]
        + [pltpu.VMEM((count, R), jnp.bfloat16)] * 4,
        name="last_update",
    )(left_sums, weight, range_grad, *rest)


def hand_over_dp(value):
    return lax.all_to_all(value, "dp", 0, 0, tiled=True)


def body(acts, grads_out, sketch_in, sketch_out, weight_grad):
    tokens_all = acts.shape[0] * lax.axis_size("dp")
    columns = weight_grad.shape[1]
    core_id = lax.axis_index("tensor") % 2
    places = jnp.stack([tensor_chunk(), core_id]).astype(jnp.int32)
    width = R // 8

    part, sq_one = sketches(1 - core_id, grads_out, acts, sketch_out, sketch_in)
    other = swap_cores(part)
    part, sq_two = sketches(core_id, grads_out, acts, sketch_out, sketch_in)
    own = gather_four(scatter_four(part + other, "x"), "x")
    other = swap_cores(own)

    part, core = range_act_of(places, own, other, acts, tokens_all)
    part = hand_over_dp(part)
    first, second, piece = range_grad_of(
        places, own, other, grads_out, sq_one, sq_two, part, tokens_all
    )

    moves = []
    for d in range(16):
        for t in range(8):
            k = d % 8
            moves.append((d * 8 + t, (2 * t + d // 8) * 8 + 2 * (k % 4) + k // 4))
    piece = lax.ppermute(piece, ("dp", "tensor"), moves)
    rows_act = gather_tensor(piece)

    piece = scatter_dp_after(first, second, rows_act)
    range_grad = lax.all_gather(piece, "dp", axis=0, tiled=True)

    piece = scatter_dp(*left_products(places, rows_act, core, weight_grad))
    left_sums = lax.all_gather(piece, "dp", axis=0, tiled=True)
    small = gather_tensor(piece[:, columns:])
    small = hand_over_dp(pack(pack_small_kernel, small, 512, "pack_small"))

    part = scatter_tensor(right_products(range_grad, weight_grad, piece))
    extra = range_grad[:, columns:]
    rest = jnp.pad(extra[:8], ((0, 0), (0, R - 128)))
    right = gather_tensor(jnp.concatenate([part, extra[:, :width].T, rest]))
    both = hand_over_dp(pack(pack_both_kernel, right, R, "pack_both"))

    counts = (float(tokens_all * FF), float(tokens_all * D))
    inverse_act, inverse_grad, scale = factors(right, small, counts)
    return last_update(
        left_sums, weight_grad, range_grad, right, both, rows_act, inverse_act, inverse_grad, scale
    )


def solution(mesh):
    return jax.shard_map(
        body,
        mesh=mesh,
        in_specs=(
            P("dp", "tensor"),
            P("dp", "tensor"),
            P("tensor", None),
            P("tensor", None),
            P("dp", "tensor"),
        ),
        out_specs=P("dp", "tensor"),
        check_vma=False,
    )
```

profile of v0, /device:TPU:1, one launch (start us, length us, event | category | flops | bytes accessed | tf_op | source)
XLA Modules:
  0.0 334.4 jit_solution(11052601194901149930)
XLA Ops:
  6.5 6.3 %sketches.3 = (f32[768,512]{1,0:T(8,128)}, f32[16,128]{1,0:T(8,128)}) custom-call(s32[1]{0:T(128)} %bitcast.2.core, bf16[1536,3072]{1,0:T(8,128)(2,1)} %grads.5, bf16[1536,768]{1,0:T(8,128)(2,1)} %acts.5, bf16[3072,256]{1,0:T(8,128)(2,1)} %sketch_out.3, bf16[768,256]{1,0:T(8,128)(2,1)} %sketch_in.3), custom_call_target="tpu_custom_call" | custom-call | tf_op jit(solution)/shard_map/sketches/pallas_call | solution.py:203
  12.8 1.4 collective-permute-start
  14.2 6.3 %sketches.2 = (f32[768,512]{1,0:T(8,128)}, f32[16,128]{1,0:T(8,128)}) custom-call(s32[1]{0:T(128)} %bitcast.1.core, bf16[1536,3072]{1,0:T(8,128)(2,1)} %grads.5, bf16[1536,768]{1,0:T(8,128)(2,1)} %acts.5, bf16[3072,256]{1,0:T(8,128)(2,1)} %sketch_out.3, bf16[768,256]{1,0:T(8,128)(2,1)} %sketch_in.3), custom_call_target="tpu_custom_call" | custom-call | tf_op jit(solution)/shard_map/sketches/pallas_call | solution.py:203
  20.5 1.8 add.365
  22.4 2.9 collective-permute-start.1
  26.8 7.9 %collective-permute-done.1 = f32[192,512]{1,0:T(8,128)S(1)} collective-permute-done((f32[192,512]{1,0:T(8,128)S(1)}, f32[192,512]{1,0:T(8,128)S(1)}, u32[]{:S(2)}, u32[]{:S(2)}) %collective-permute-start.1) | collective-permute-done | bytes 393248 | tf_op jit(solution)/shard_map/ppermute | solution.py:29
  34.7 8.7 %collective-permute-done.3 = f32[192,512]{1,0:T(8,128)S(1)} collective-permute-done((f32[192,512]{1,0:T(8,128)S(1)}, f32[192,512]{1,0:T(8,128)S(1)}, u32[]{:S(2)}, u32[]{:S(2)}) %collective-permute-start.3) | collective-permute-done | bytes 393248 | tf_op jit(solution)/shard_map/ppermute | solution.py:29
  45.1 1.3 constant_dynamic-update-slice_fusion.15
  46.4 1.5 collective-permute-start.4
  48.0 2.3 collective-permute-start.5
  50.8 6.8 %collective-permute-done.4 = f32[192,512]{1,0:T(8,128)S(1)} collective-permute-done((f32[192,512]{1,0:T(8,128)S(1)}, f32[192,512]{1,0:T(8,128)S(1)}, u32[]{:S(2)}, u32[]{:S(2)}) %collective-permute-start.4) | collective-permute-done | bytes 393248 | tf_op jit(solution)/shard_map/ppermute | solution.py:29
  57.6 9.9 %collective-permute-done.5 = f32[192,512]{1,0:T(8,128)S(1)} collective-permute-done((f32[192,512]{1,0:T(8,128)S(1)}, f32[192,512]{1,0:T(8,128)S(1)}, u32[]{:S(2)}, u32[]{:S(2)}) %collective-permute-start.5) | collective-permute-done | bytes 393248 | tf_op jit(solution)/shard_map/ppermute | solution.py:29
  67.6 1.4 collective-permute-start.7
  69.6 2.4 collective-permute-done.7.other
  72.0 1.2 copy-done.1
  73.2 5.6 %range_act.1 = (f32[768,256]{1,0:T(8,128)}, f32[256,128]{1,0:T(8,128)}) custom-call(s32[2]{0:T(128)} %pad_add_fusion.place_ref, f32[768,512]{1,0:T(8,128)} %copy-done, f32[768,512]{1,0:T(8,128)} %copy-done.1, bf16[1536,768]{1,0:T(8,128)(2,1)} %acts.5), custom_call_target="tpu_custom_call" | custom-call | tf_op jit(solution)/shard_map/range_act/pallas_call | solution.py:301
  78.8 7.8 %all-to-all-start = ((f32[16,48,256]{2,1,0:T(8,128)}), f32[16,48,256]{2,1,0:T(8,128)S(1)}, u32[]{:S(2)}, u32[]{:S(2)}) async-start(f32[16,48,256]{2,1,0:T(8,128)} %bitcast.18), calls=%async_computation | async-start | bytes 1572864 | tf_op jit(solution)/shard_map/all_to_all | solution.py:554
  86.8 13.2 %all-to-all-done = f32[16,48,256]{2,1,0:T(8,128)S(1)} async-done(((f32[16,48,256]{2,1,0:T(8,128)}), f32[16,48,256]{2,1,0:T(8,128)S(1)}, u32[]{:S(2)}, u32[]{:S(2)}) %all-to-all-start) | async-done | bytes 786464 | tf_op jit(solution)/shard_map/all_to_all | solution.py:554
  101.0 11.3 %range_grad.1 = (f32[128,3200]{1,0:T(8,128)}, f32[128,3200]{1,0:T(8,128)}, f32[48,256]{1,0:T(8,128)}) custom-call(s32[2]{0:T(128)} %pad_add_fusion.place_ref, f32[768,512]{1,0:T(8,128)} %copy-done, f32[768,512]{1,0:T(8,128)} %copy-done.1, bf16[1536,3072]{1,0:T(8,128)(2,1)} %grads.5, f32[16,128]{1,0:T(8,128)} %get-tuple-element.21.sq_one, ...), custom_call_target="tpu_custom_call" | custom-call | tf_op jit(solution)/shard_map/range_grad/pallas_call | solution.py:272
  112.2 4.2 %collective-permute-start.8 = (f32[48,256]{1,0:T(8,128)}, f32[48,256]{1,0:T(8,128)S(1)}, u32[]{:S(2)}, u32[]{:S(2)}) collective-permute-start(f32[48,256]{1,0:T(8,128)} %get-tuple-element.24), channel_id=1, source_target_pairs={{0,0},{1,16},{2,32},{3,48},{4,64},{5,80},{6,96},{7,112},{8,2},{9,1... | collective-permute-start | bytes 147464 | tf_op jit(solution)/shard_map/ppermute | solution.py:581
  116.5 1.3 constant_dynamic-slice_fusion.13
  117.8 1.9 collective-permute-start.27
  119.7 1.3 collective-permute-start.25
  121.0 3.0 collective-permute-start.11
  124.1 4.4 %collective-permute-done.9 = f32[48,256]{1,0:T(8,128)S(1)} collective-permute-done((f32[48,256]{1,0:T(8,128)S(1)}, f32[48,256]{1,0:T(8,128)S(1)}, u32[]{:S(2)}, u32[]{:S(2)}) %collective-permute-start.9) | collective-permute-done | bytes 49184 | tf_op jit(solution)/shard_map/ppermute | solution.py:29
  128.5 4.4 %collective-permute-done.10 = f32[48,256]{1,0:T(8,128)S(1)} collective-permute-done((f32[48,256]{1,0:T(8,128)S(1)}, f32[48,256]{1,0:T(8,128)S(1)}, u32[]{:S(2)}, u32[]{:S(2)}) %collective-permute-start.10) | collective-permute-done | bytes 49184 | tf_op jit(solution)/shard_map/ppermute | solution.py:29
  132.9 4.0 %collective-permute-start.12 = (f32[192,256]{1,0:T(8,128)S(1)}, f32[192,256]{1,0:T(8,128)S(1)}, u32[]{:S(2)}, u32[]{:S(2)}) collective-permute-start(f32[192,256]{1,0:T(8,128)S(1)} %constant_dynamic-update-slice_fusion.8), channel_id=1, source_target_pairs={{0,1},{1,0},{2,3},{3,2},{4,5},{5,4},{6,7},{7,6},{8,9},{9,8},{10,11... | collective-permute-start | bytes 589832 | tf_op jit(solution)/shard_map/ppermute | solution.py:33
  139.6 2.1 collective-permute-start.31
  142.7 2.2 sum_blocks.2
  146.8 1.9 collective-permute-start.30
  149.9 9.1 %collective-permute-done.31.two = f32[32,3200]{1,0:T(8,128)S(1)} collective-permute-done((f32[32,3200]{1,0:T(8,128)S(1)}, f32[32,3200]{1,0:T(8,128)S(1)}, u32[]{:S(2)}, u32[]{:S(2)}) %collective-permute-start.31) | collective-permute-done | bytes 409632 | tf_op jit(solution)/shard_map/ppermute | solution.py:29
  159.8 2.2 sum_blocks.3
  163.8 6.6 %collective-permute-start.36 = (f32[8,3200]{1,0:T(8,128)S(1)}, f32[8,3200]{1,0:T(8,128)S(1)}, u32[]{:S(2)}, u32[]{:S(2)}) collective-permute-start(f32[8,3200]{1,0:T(8,128)S(1)} %get-tuple-element.58), channel_id=1, source_target_pairs={{0,24},{8,0},{16,8},{24,16},{32,56},{40,32},{48,40},{56,48},{64,88... | collective-permute-start | bytes 307208 | tf_op jit(solution)/shard_map/ppermute | solution.py:29
  171.4 1.3 collective-permute-done.36
  172.7 2.5 collective-permute-done.35
  176.9 8.7 %left_products.1 = (f32[128,3200]{1,0:T(8,128)}, f32[128,3200]{1,0:T(8,128)}) custom-call(s32[2]{0:T(128)} %pad_add_fusion.place_ref, f32[384,256]{1,0:T(8,128)} %pad_maximum_fusion.1.rows_act.after, f32[256,128]{1,0:T(8,128)} %get-tuple-element.25.core, f32[384,3072]{1,0:T(8,128)} %weight.5), custom_call_target="tpu_custom_call" | custom-call | tf_op jit(solution)/shard_map/left_products/pallas_call | solution.py:344
  185.6 1.5 constant_dynamic-slice_fusion.27
  187.1 1.5 collective-permute-start.15
  188.9 10.1 %collective-permute-done.13 = f32[32,3200]{1,0:T(8,128)S(1)} collective-permute-done((f32[32,3200]{1,0:T(8,128)S(1)}, f32[32,3200]{1,0:T(8,128)S(1)}, u32[]{:S(2)}, u32[]{:S(2)}) %collective-permute-start.13) | collective-permute-done | bytes 409632 | tf_op jit(solution)/shard_map/ppermute | solution.py:29
  199.0 8.7 %collective-permute-done.15 = f32[32,3200]{1,0:T(8,128)S(1)} collective-permute-done((f32[32,3200]{1,0:T(8,128)S(1)}, f32[32,3200]{1,0:T(8,128)S(1)}, u32[]{:S(2)}, u32[]{:S(2)}) %collective-permute-start.15) | collective-permute-done | bytes 409632 | tf_op jit(solution)/shard_map/ppermute | solution.py:29
  207.8 2.6 collective-permute-done.14
  212.2 1.4 collective-permute-start.17
  215.2 4.5 %collective-permute-done.16 = f32[8,3200]{1,0:T(8,128)S(1)} collective-permute-done((f32[8,3200]{1,0:T(8,128)S(1)}, f32[8,3200]{1,0:T(8,128)S(1)}, u32[]{:S(2)}, u32[]{:S(2)}) %collective-permute-start.16) | collective-permute-done | bytes 102432 | tf_op jit(solution)/shard_map/ppermute | solution.py:29
  219.8 2.5 collective-permute-done.18
  222.4 3.1 collective-permute-done.23
  226.3 6.8 %all-gather.5.cloned.1.call-done.whole.range_grad = f32[256,3200]{1,0:T(8,128)} async-done(((f32[16,3200]{1,0:T(8,128)}), f32[256,3200]{1,0:T(8,128)}) %all-gather.5.cloned.1.call-update) | async-done | bytes 3276816 | tf_op jit(solution)/shard_map/all_gather | solution.py:585
  233.1 8.6 %right_products.1 = f32[704,256]{1,0:T(8,128)} custom-call(f32[256,3200]{1,0:T(8,128)} %all-gather.5.cloned.1.call-done.whole.range_grad, f32[384,3072]{1,0:T(8,128)} %weight.5, f32[16,3200]{1,0:T(8,128)} %pad_maximum_fusion.2.left), custom_call_target="tpu_custom_call" | custom-call | tf_op jit(solution)/shard_map/right_products/pallas_call | solution.py:370
  243.8 1.2 collective-permute-start.46
  246.2 1.8 collective-permute-start.38
  248.1 1.9 collective-permute-start.40
  251.7 13.2 %collective-permute-start.47 = (f32[16,128]{1,0:T(8,128)S(1)}, f32[16,128]{1,0:T(8,128)S(1)}, u32[]{:S(2)}, u32[]{:S(2)}) collective-permute-start(f32[16,128]{1,0:T(8,128)S(1)} %get-tuple-element.34), channel_id=1, source_target_pairs={{0,6},{1,7},{2,0},{3,1},{4,2},{5,3},{6,4},{7,5},{8,14},{9,15},{10,... | collective-permute-start | bytes 24584 | tf_op jit(solution)/shard_map/ppermute | solution.py:29
  265.1 1.2 collective-permute-start.42
  266.3 1.6 collective-permute-start.43
  267.9 4.1 %collective-permute-done.41 = f32[128,256]{1,0:T(8,128)S(1)} collective-permute-done((f32[128,256]{1,0:T(8,128)S(1)}, f32[128,256]{1,0:T(8,128)S(1)}, u32[]{:S(2)}, u32[]{:S(2)}) %collective-permute-start.41) | collective-permute-done | bytes 131104 | tf_op jit(solution)/shard_map/ppermute | solution.py:29
  272.6 3.4 %collective-permute-start.44 = (f32[512,256]{1,0:T(8,128)S(1)}, f32[512,256]{1,0:T(8,128)S(1)}, u32[]{:S(2)}, u32[]{:S(2)}) collective-permute-start(f32[512,256]{1,0:T(8,128)S(1)} %constant_dynamic-update-slice_fusion.4), channel_id=1, source_target_pairs={{0,1},{1,0},{2,3},{3,2},{4,5},{5,4},{6,7},{7,6},{8,9},{9,8},{10,11... | collective-permute-start | bytes 1572872 | tf_op jit(solution)/shard_map/ppermute | solution.py:33
  276.0 1.5 collective-permute-done.48
  278.1 1.8 pack_small.1
  279.9 4.5 %all-to-all-start.2 = ((f32[16,32,256]{2,1,0:T(8,128)}), f32[16,32,256]{2,1,0:T(8,128)S(1)}, u32[]{:S(2)}, u32[]{:S(2)}) async-start(f32[16,32,256]{2,1,0:T(8,128)} %bitcast.15), calls=%async_computation.2 | async-start | bytes 1048576 | tf_op jit(solution)/shard_map/all_to_all | solution.py:554
  284.5 1.1 pad_maximum_fusion.right
  285.6 2.0 pack_both.1
  287.6 7.5 %all-to-all-done.2 = f32[16,32,256]{2,1,0:T(8,128)S(1)} async-done(((f32[16,32,256]{2,1,0:T(8,128)}), f32[16,32,256]{2,1,0:T(8,128)S(1)}, u32[]{:S(2)}, u32[]{:S(2)}) %all-to-all-start.2) | async-done | bytes 524320 | tf_op jit(solution)/shard_map/all_to_all | solution.py:554
  295.1 3.5 %all-to-all-start.1 = ((f32[16,16,256]{2,1,0:T(8,128)}), f32[16,16,256]{2,1,0:T(8,128)S(1)}, u32[]{:S(2)}, u32[]{:S(2)}) async-start(f32[16,16,256]{2,1,0:T(8,128)} %bitcast.17), calls=%async_computation.1 | async-start | bytes 524288 | tf_op jit(solution)/shard_map/all_to_all | solution.py:554
  298.6 16.3 %factors.1 = (f32[256,256]{1,0:T(8,128)}, f32[256,256]{1,0:T(8,128)}, f32[8,128]{1,0:T(8,128)}) custom-call(f32[1024,256]{1,0:T(8,128)} %pad_maximum_fusion.right, f32[512,256]{1,0:T(8,128)} %bitcast.14), custom_call_target="tpu_custom_call" | custom-call | tf_op jit(solution)/shard_map/factors/pallas_call | solution.py:500
  315.6 11.7 %last_update.1 = f32[384,3072]{1,0:T(8,128)} custom-call(f32[256,3200]{1,0:T(8,128)} %all-gather.3.cloned.1.call-done.left_sums, f32[384,3072]{1,0:T(8,128)} %weight.5, f32[256,3200]{1,0:T(8,128)} %all-gather.5.cloned.1.call-done.whole.range_grad, f32[1024,256]{1,0:T(8,128)} %pad_maximum_fusion.right, f32[256,256]{1,0:T(8,128)} %bitcast.16, ...), custom_call_target="tpu_custom_call" | custom-call | tf_op jit(solution)/shard_map/last_update/pallas_call | solution.py:536
  (142 shorter events, 29.7 us)
Async XLA Ops:
  12.8 7.7 %collective-permute-start = (f32[768,512]{1,0:T(8,128)}, f32[768,512]{1,0:T(8,128)S(1)}, u32[]{:S(2)}, u32[]{:S(2)}) collective-permute-start(f32[768,512]{1,0:T(8,128)} %get-tuple-element.20), channel_id=1, source_target_pairs={{0,1},{1,0},{2,3},{3,2},{4,5},{5,4},{6,7},{7,6},{8,9},{9,8},{10,11... | collective-permute-start | bytes 4718600 | tf_op jit(solution)/shard_map/ppermute | solution.py:33
  22.4 12.3 %collective-permute-start.1 = (f32[192,512]{1,0:T(8,128)S(1)}, f32[192,512]{1,0:T(8,128)S(1)}, u32[]{:S(2)}, u32[]{:S(2)}) collective-permute-start(f32[192,512]{1,0:T(8,128)S(1)} %get-tuple-element.49), channel_id=1, source_target_pairs={{0,4},{1,5},{2,6},{3,7},{4,0},{5,1},{6,2},{7,3},{8,12},{9,13},{10,... | collective-permute-start | bytes 1179656 | tf_op jit(solution)/shard_map/ppermute | solution.py:29
  25.3 18.1 %collective-permute-start.3 = (f32[192,512]{1,0:T(8,128)S(1)}, f32[192,512]{1,0:T(8,128)S(1)}, u32[]{:S(2)}, u32[]{:S(2)}) collective-permute-start(f32[192,512]{1,0:T(8,128)S(1)} %get-tuple-element.50), channel_id=1, source_target_pairs={{0,6},{1,7},{2,0},{3,1},{4,2},{5,3},{6,4},{7,5},{8,14},{9,15},{10,... | collective-permute-start | bytes 1179656 | tf_op jit(solution)/shard_map/ppermute | solution.py:29
  26.2 17.4 %collective-permute-start.2 = (f32[192,512]{1,0:T(8,128)S(1)}, f32[192,512]{1,0:T(8,128)}, u32[]{:S(2)}, u32[]{:S(2)}) collective-permute-start(f32[192,512]{1,0:T(8,128)S(1)} %get-tuple-element.51), channel_id=1, source_target_pairs={{0,2},{1,3},{2,4},{3,5},{4,6},{5,7},{6,0},{7,1},{8,10},{9,11},{10,... | collective-permute-start | bytes 1179656 | tf_op jit(solution)/shard_map/ppermute | solution.py:29
  34.7 8.7 %copy-start.13 = (f32[192,512]{1,0:T(8,128)}, f32[192,512]{1,0:T(8,128)S(1)}, u32[]{:S(2)}) copy-start(f32[192,512]{1,0:T(8,128)S(1)} %collective-permute-done.1) | copy-start | bytes 1179652
  44.1 1.0 copy-start.14
  46.4 11.2 %collective-permute-start.4 = (f32[192,512]{1,0:T(8,128)S(1)}, f32[192,512]{1,0:T(8,128)S(1)}, u32[]{:S(2)}, u32[]{:S(2)}) collective-permute-start(f32[192,512]{1,0:T(8,128)S(1)} %get-tuple-element.36), channel_id=1, source_target_pairs={{0,2},{1,3},{2,4},{3,5},{4,6},{5,7},{6,0},{7,1},{8,10},{9,11},{10,... | collective-permute-start | bytes 1179656 | tf_op jit(solution)/shard_map/ppermute | solution.py:29
  48.0 19.5 %collective-permute-start.5 = (f32[192,512]{1,0:T(8,128)S(1)}, f32[192,512]{1,0:T(8,128)S(1)}, u32[]{:S(2)}, u32[]{:S(2)}) collective-permute-start(f32[192,512]{1,0:T(8,128)S(1)} %get-tuple-element.36), channel_id=1, source_target_pairs={{0,4},{1,5},{2,6},{3,7},{4,0},{5,1},{6,2},{7,3},{8,12},{9,13},{10,... | collective-permute-start | bytes 1179656 | tf_op jit(solution)/shard_map/ppermute | solution.py:29
  50.3 17.2 %collective-permute-start.6 = (f32[192,512]{1,0:T(8,128)S(1)}, f32[192,512]{1,0:T(8,128)S(1)}, u32[]{:S(2)}, u32[]{:S(2)}) collective-permute-start(f32[192,512]{1,0:T(8,128)S(1)} %get-tuple-element.36), channel_id=1, source_target_pairs={{0,6},{1,7},{2,0},{3,1},{4,2},{5,3},{6,4},{7,5},{8,14},{9,15},{10,... | collective-permute-start | bytes 1179656 | tf_op jit(solution)/shard_map/ppermute | solution.py:29
  67.6 4.4 %copy-start = (f32[768,512]{1,0:T(8,128)}, f32[768,512]{1,0:T(8,128)S(1)}, u32[]{:S(2)}) copy-start(f32[768,512]{1,0:T(8,128)S(1)} %constant_dynamic-update-slice_fusion.12.own) | copy-start | bytes 4718596
  67.6 4.4 %collective-permute-start.7 = (f32[768,512]{1,0:T(8,128)S(1)}, f32[768,512]{1,0:T(8,128)S(1)}, u32[]{:S(2)}, u32[]{:S(2)}) collective-permute-start(f32[768,512]{1,0:T(8,128)S(1)} %constant_dynamic-update-slice_fusion.12.own), channel_id=1, source_target_pairs={{0,1},{1,0},{2,3},{3,2},{4,5},{5,4},{6,7},{7,6},{8,9},{9,8},{10,11... | collective-permute-start | bytes 4718600 | tf_op jit(solution)/shard_map/ppermute | solution.py:33
  72.0 1.2 copy-start.1
  78.8 21.3 %all-to-all-start = ((f32[16,48,256]{2,1,0:T(8,128)}), f32[16,48,256]{2,1,0:T(8,128)S(1)}, u32[]{:S(2)}, u32[]{:S(2)}) async-start(f32[16,48,256]{2,1,0:T(8,128)} %bitcast.18), calls=%async_computation | async-start | bytes 1572864 | tf_op jit(solution)/shard_map/all_to_all | solution.py:554
  86.5 146.6 %all-gather.5.cloned.1.call-start = ((), (), s32[]{:S(2)}) async-start(), calls=%async_computation.4 | async-start | bytes 3481600 | tf_op jit(solution)/shard_map/all_gather | solution.py:585
  112.2 24.7 %copy-start.2 = (f32[128,3200]{1,0:T(8,128)S(1)}, f32[128,3200]{1,0:T(8,128)}, u32[]{:S(2)}) copy-start(f32[128,3200]{1,0:T(8,128)} %get-tuple-element.29.value) | copy-start | bytes 4915204
  112.2 8.8 %collective-permute-start.8 = (f32[48,256]{1,0:T(8,128)}, f32[48,256]{1,0:T(8,128)S(1)}, u32[]{:S(2)}, u32[]{:S(2)}) collective-permute-start(f32[48,256]{1,0:T(8,128)} %get-tuple-element.24), channel_id=1, source_target_pairs={{0,0},{1,16},{2,32},{3,48},{4,64},{5,80},{6,96},{7,112},{8,2},{9,1... | collective-permute-start | bytes 147464 | tf_op jit(solution)/shard_map/ppermute | solution.py:581
  117.8 21.8 %collective-permute-start.27 = (f32[32,3200]{1,0:T(8,128)S(1)}, f32[32,3200]{1,0:T(8,128)S(1)}, u32[]{:S(2)}, u32[]{:S(2)}) collective-permute-start(f32[32,3200]{1,0:T(8,128)S(1)} %get-tuple-element.37), channel_id=1, source_target_pairs={{0,24},{8,0},{16,8},{24,16},{32,56},{40,32},{48,40},{56,48},{64,88... | collective-permute-start | bytes 1228808 | tf_op jit(solution)/shard_map/ppermute | solution.py:29
  119.7 22.1 %collective-permute-start.26 = (f32[32,3200]{1,0:T(8,128)S(1)}, f32[32,3200]{1,0:T(8,128)S(1)}, u32[]{:S(2)}, u32[]{:S(2)}) collective-permute-start(f32[32,3200]{1,0:T(8,128)S(1)} %get-tuple-element.38), channel_id=1, source_target_pairs={{0,8},{8,16},{16,24},{24,0},{32,40},{40,48},{48,56},{56,32},{64,72... | collective-permute-start | bytes 1228808 | tf_op jit(solution)/shard_map/ppermute | solution.py:29
  119.7 22.1 %collective-permute-start.25 = (f32[32,3200]{1,0:T(8,128)S(1)}, f32[32,3200]{1,0:T(8,128)S(1)}, u32[]{:S(2)}, u32[]{:S(2)}) collective-permute-start(f32[32,3200]{1,0:T(8,128)S(1)} %get-tuple-element.39), channel_id=1, source_target_pairs={{0,16},{8,24},{16,0},{24,8},{32,48},{40,56},{48,32},{56,40},{64,80... | collective-permute-start | bytes 1228808 | tf_op jit(solution)/shard_map/ppermute | solution.py:29
  121.0 11.9 %collective-permute-start.11 = (f32[48,256]{1,0:T(8,128)S(1)}, f32[48,256]{1,0:T(8,128)S(1)}, u32[]{:S(2)}, u32[]{:S(2)}) collective-permute-start(f32[48,256]{1,0:T(8,128)S(1)} %collective-permute-done.8), channel_id=1, source_target_pairs={{0,6},{1,7},{2,0},{3,1},{4,2},{5,3},{6,4},{7,5},{8,14},{9,15},{10,... | collective-permute-start | bytes 147464 | tf_op jit(solution)/shard_map/ppermute | solution.py:29
  124.0 4.4 %collective-permute-start.9 = (f32[48,256]{1,0:T(8,128)S(1)}, f32[48,256]{1,0:T(8,128)S(1)}, u32[]{:S(2)}, u32[]{:S(2)}) collective-permute-start(f32[48,256]{1,0:T(8,128)S(1)} %collective-permute-done.8), channel_id=1, source_target_pairs={{0,2},{1,3},{2,4},{3,5},{4,6},{5,7},{6,0},{7,1},{8,10},{9,11},{10,... | collective-permute-start | bytes 147464 | tf_op jit(solution)/shard_map/ppermute | solution.py:29
  128.5 4.4 %collective-permute-start.10 = (f32[48,256]{1,0:T(8,128)S(1)}, f32[48,256]{1,0:T(8,128)S(1)}, u32[]{:S(2)}, u32[]{:S(2)}) collective-permute-start(f32[48,256]{1,0:T(8,128)S(1)} %collective-permute-done.8), channel_id=1, source_target_pairs={{0,4},{1,5},{2,6},{3,7},{4,0},{5,1},{6,2},{7,3},{8,12},{9,13},{10,... | collective-permute-start | bytes 147464 | tf_op jit(solution)/shard_map/ppermute | solution.py:29
  132.9 5.0 %collective-permute-start.12 = (f32[192,256]{1,0:T(8,128)S(1)}, f32[192,256]{1,0:T(8,128)S(1)}, u32[]{:S(2)}, u32[]{:S(2)}) collective-permute-start(f32[192,256]{1,0:T(8,128)S(1)} %constant_dynamic-update-slice_fusion.8), channel_id=1, source_target_pairs={{0,1},{1,0},{2,3},{3,2},{4,5},{5,4},{6,7},{7,6},{8,9},{9,8},{10,11... | collective-permute-start | bytes 589832 | tf_op jit(solution)/shard_map/ppermute | solution.py:33
  137.0 11.7 %collective-permute-start.33 = (f32[32,3200]{1,0:T(8,128)S(1)}, f32[32,3200]{1,0:T(8,128)S(1)}, u32[]{:S(2)}, u32[]{:S(2)}) collective-permute-start(f32[32,3200]{1,0:T(8,128)S(1)} %get-tuple-element.40), channel_id=1, source_target_pairs={{0,96},{8,104},{16,112},{24,120},{32,0},{40,8},{48,16},{56,24},{64... | collective-permute-start | bytes 1228808 | tf_op jit(solution)/shard_map/ppermute | solution.py:29
  138.0 11.9 %collective-permute-start.32 = (f32[32,3200]{1,0:T(8,128)S(1)}, f32[32,3200]{1,0:T(8,128)S(1)}, u32[]{:S(2)}, u32[]{:S(2)}) collective-permute-start(f32[32,3200]{1,0:T(8,128)S(1)} %get-tuple-element.41), channel_id=1, source_target_pairs={{0,32},{8,40},{16,48},{24,56},{32,64},{40,72},{48,80},{56,88},{64,... | collective-permute-start | bytes 1228808 | tf_op jit(solution)/shard_map/ppermute | solution.py:29
  139.6 2.2 copy-start.7
  139.6 19.4 %collective-permute-start.31 = (f32[32,3200]{1,0:T(8,128)S(1)}, f32[32,3200]{1,0:T(8,128)S(1)}, u32[]{:S(2)}, u32[]{:S(2)}) collective-permute-start(f32[32,3200]{1,0:T(8,128)S(1)} %get-tuple-element.42), channel_id=1, source_target_pairs={{0,64},{8,72},{16,80},{24,88},{32,96},{40,104},{48,112},{56,120},{... | collective-permute-start | bytes 1228808 | tf_op jit(solution)/shard_map/ppermute | solution.py:29
  145.9 24.5 %collective-permute-start.28 = (f32[8,3200]{1,0:T(8,128)S(1)}, f32[8,3200]{1,0:T(8,128)S(1)}, u32[]{:S(2)}, u32[]{:S(2)}) collective-permute-start(f32[8,3200]{1,0:T(8,128)S(1)} %get-tuple-element.54), channel_id=1, source_target_pairs={{0,64},{8,72},{16,80},{24,88},{32,96},{40,104},{48,112},{56,120},{... | collective-permute-start | bytes 307208 | tf_op jit(solution)/shard_map/ppermute | solution.py:29
  146.8 23.6 %collective-permute-start.30 = (f32[8,3200]{1,0:T(8,128)S(1)}, f32[8,3200]{1,0:T(8,128)S(1)}, u32[]{:S(2)}, u32[]{:S(2)}) collective-permute-start(f32[8,3200]{1,0:T(8,128)S(1)} %get-tuple-element.55), channel_id=1, source_target_pairs={{0,96},{8,104},{16,112},{24,120},{32,0},{40,8},{48,16},{56,24},{64... | collective-permute-start | bytes 307208 | tf_op jit(solution)/shard_map/ppermute | solution.py:29
  148.7 10.3 %copy-start.10 = (f32[32,3200]{1,0:T(8,128)}, f32[32,3200]{1,0:T(8,128)S(1)}, u32[]{:S(2)}) copy-start(f32[32,3200]{1,0:T(8,128)S(1)} %collective-permute-done.33.three) | copy-start | bytes 1228804
  148.7 21.8 %collective-permute-start.29 = (f32[8,3200]{1,0:T(8,128)S(1)}, f32[8,3200]{1,0:T(8,128)S(1)}, u32[]{:S(2)}, u32[]{:S(2)}) collective-permute-start(f32[8,3200]{1,0:T(8,128)S(1)} %get-tuple-element.56), channel_id=1, source_target_pairs={{0,32},{8,40},{16,48},{24,56},{32,64},{40,72},{48,80},{56,88},{64,... | collective-permute-start | bytes 307208 | tf_op jit(solution)/shard_map/ppermute | solution.py:29
  149.9 9.2 %copy-start.11 = (f32[32,3200]{1,0:T(8,128)}, f32[32,3200]{1,0:T(8,128)S(1)}, u32[]{:S(2)}) copy-start(f32[32,3200]{1,0:T(8,128)S(1)} %collective-permute-done.32.one) | copy-start | bytes 1228804
  163.0 8.4 %collective-permute-start.34 = (f32[8,3200]{1,0:T(8,128)S(1)}, f32[8,3200]{1,0:T(8,128)S(1)}, u32[]{:S(2)}, u32[]{:S(2)}) collective-permute-start(f32[8,3200]{1,0:T(8,128)S(1)} %get-tuple-element.57), channel_id=1, source_target_pairs={{0,16},{8,24},{16,0},{24,8},{32,48},{40,56},{48,32},{56,40},{64,80... | collective-permute-start | bytes 307208 | tf_op jit(solution)/shard_map/ppermute | solution.py:29
  163.8 8.8 %collective-permute-start.36 = (f32[8,3200]{1,0:T(8,128)S(1)}, f32[8,3200]{1,0:T(8,128)S(1)}, u32[]{:S(2)}, u32[]{:S(2)}) collective-permute-start(f32[8,3200]{1,0:T(8,128)S(1)} %get-tuple-element.58), channel_id=1, source_target_pairs={{0,24},{8,0},{16,8},{24,16},{32,56},{40,32},{48,40},{56,48},{64,88... | collective-permute-start | bytes 307208 | tf_op jit(solution)/shard_map/ppermute | solution.py:29
  170.5 4.7 %collective-permute-start.35 = (f32[8,3200]{1,0:T(8,128)S(1)}, f32[8,3200]{1,0:T(8,128)S(1)}, u32[]{:S(2)}, u32[]{:S(2)}) collective-permute-start(f32[8,3200]{1,0:T(8,128)S(1)} %get-tuple-element.59), channel_id=1, source_target_pairs={{0,8},{8,16},{16,24},{24,0},{32,40},{40,48},{48,56},{56,32},{64,72... | collective-permute-start | bytes 307208 | tf_op jit(solution)/shard_map/ppermute | solution.py:29
  176.8 138.1 %all-gather.3.cloned.1.call-start = ((), (), s32[]{:S(2)}) async-start(), calls=%async_computation.3 | async-start | bytes 3481600 | tf_op jit(solution)/shard_map/all_gather | solution.py:588
  185.6 3.1 copy-start.5
  187.0 12.0 %collective-permute-start.13 = (f32[32,3200]{1,0:T(8,128)S(1)}, f32[32,3200]{1,0:T(8,128)S(1)}, u32[]{:S(2)}, u32[]{:S(2)}) collective-permute-start(f32[32,3200]{1,0:T(8,128)S(1)} %get-tuple-element.43), channel_id=1, source_target_pairs={{0,16},{8,24},{16,0},{24,8},{32,48},{40,56},{48,32},{56,40},{64,80... | collective-permute-start | bytes 1228808 | tf_op jit(solution)/shard_map/ppermute | solution.py:29
  187.1 20.7 %collective-permute-start.15 = (f32[32,3200]{1,0:T(8,128)S(1)}, f32[32,3200]{1,0:T(8,128)S(1)}, u32[]{:S(2)}, u32[]{:S(2)}) collective-permute-start(f32[32,3200]{1,0:T(8,128)S(1)} %get-tuple-element.44), channel_id=1, source_target_pairs={{0,24},{8,0},{16,8},{24,16},{32,56},{40,32},{48,40},{56,48},{64,88... | collective-permute-start | bytes 1228808 | tf_op jit(solution)/shard_map/ppermute | solution.py:29
  188.6 21.8 %collective-permute-start.14 = (f32[32,3200]{1,0:T(8,128)S(1)}, f32[32,3200]{1,0:T(8,128)S(1)}, u32[]{:S(2)}, u32[]{:S(2)}) collective-permute-start(f32[32,3200]{1,0:T(8,128)S(1)} %get-tuple-element.45), channel_id=1, source_target_pairs={{0,8},{8,16},{16,24},{24,0},{32,40},{40,48},{48,56},{56,32},{64,72... | collective-permute-start | bytes 1228808 | tf_op jit(solution)/shard_map/ppermute | solution.py:29
  188.7 23.4 %collective-permute-start.19 = (f32[32,3200]{1,0:T(8,128)S(1)}, f32[32,3200]{1,0:T(8,128)S(1)}, u32[]{:S(2)}, u32[]{:S(2)}) collective-permute-start(f32[32,3200]{1,0:T(8,128)S(1)} %get-tuple-element.46), channel_id=1, source_target_pairs={{0,64},{8,72},{16,80},{24,88},{32,96},{40,104},{48,112},{56,120},{... | collective-permute-start | bytes 1228808 | tf_op jit(solution)/shard_map/ppermute | solution.py:29
  188.9 24.6 %collective-permute-start.21 = (f32[32,3200]{1,0:T(8,128)S(1)}, f32[32,3200]{1,0:T(8,128)S(1)}, u32[]{:S(2)}, u32[]{:S(2)}) collective-permute-start(f32[32,3200]{1,0:T(8,128)S(1)} %get-tuple-element.47), channel_id=1, source_target_pairs={{0,96},{8,104},{16,112},{24,120},{32,0},{40,8},{48,16},{56,24},{64... | collective-permute-start | bytes 1228808 | tf_op jit(solution)/shard_map/ppermute | solution.py:29
  199.0 14.5 %collective-permute-start.20 = (f32[32,3200]{1,0:T(8,128)S(1)}, f32[32,3200]{1,0:T(8,128)S(1)}, u32[]{:S(2)}, u32[]{:S(2)}) collective-permute-start(f32[32,3200]{1,0:T(8,128)S(1)} %get-tuple-element.48), channel_id=1, source_target_pairs={{0,32},{8,40},{16,48},{24,56},{32,64},{40,72},{48,80},{56,88},{64,... | collective-permute-start | bytes 1228808 | tf_op jit(solution)/shard_map/ppermute | solution.py:29
  211.5 8.2 %collective-permute-start.16 = (f32[8,3200]{1,0:T(8,128)S(1)}, f32[8,3200]{1,0:T(8,128)S(1)}, u32[]{:S(2)}, u32[]{:S(2)}) collective-permute-start(f32[8,3200]{1,0:T(8,128)S(1)} %get-tuple-element.60), channel_id=1, source_target_pairs={{0,64},{8,72},{16,80},{24,88},{32,96},{40,104},{48,112},{56,120},{... | collective-permute-start | bytes 307208 | tf_op jit(solution)/shard_map/ppermute | solution.py:29
  212.1 10.2 %collective-permute-start.18 = (f32[8,3200]{1,0:T(8,128)S(1)}, f32[8,3200]{1,0:T(8,128)S(1)}, u32[]{:S(2)}, u32[]{:S(2)}) collective-permute-start(f32[8,3200]{1,0:T(8,128)S(1)} %get-tuple-element.61), channel_id=1, source_target_pairs={{0,96},{8,104},{16,112},{24,120},{32,0},{40,8},{48,16},{56,24},{64... | collective-permute-start | bytes 307208 | tf_op jit(solution)/shard_map/ppermute | solution.py:29
  212.2 10.2 %collective-permute-start.17 = (f32[8,3200]{1,0:T(8,128)S(1)}, f32[8,3200]{1,0:T(8,128)S(1)}, u32[]{:S(2)}, u32[]{:S(2)}) collective-permute-start(f32[8,3200]{1,0:T(8,128)S(1)} %get-tuple-element.62), channel_id=1, source_target_pairs={{0,32},{8,40},{16,48},{24,56},{32,64},{40,72},{48,80},{56,88},{64,... | collective-permute-start | bytes 307208 | tf_op jit(solution)/shard_map/ppermute | solution.py:29
  213.7 8.7 %collective-permute-start.22 = (f32[8,3200]{1,0:T(8,128)S(1)}, f32[8,3200]{1,0:T(8,128)S(1)}, u32[]{:S(2)}, u32[]{:S(2)}) collective-permute-start(f32[8,3200]{1,0:T(8,128)S(1)} %get-tuple-element.63), channel_id=1, source_target_pairs={{0,16},{8,24},{16,0},{24,8},{32,48},{40,56},{48,32},{56,40},{64,80... | collective-permute-start | bytes 307208 | tf_op jit(solution)/shard_map/ppermute | solution.py:29
  214.4 8.0 %collective-permute-start.24 = (f32[8,3200]{1,0:T(8,128)S(1)}, f32[8,3200]{1,0:T(8,128)S(1)}, u32[]{:S(2)}, u32[]{:S(2)}) collective-permute-start(f32[8,3200]{1,0:T(8,128)S(1)} %get-tuple-element.64), channel_id=1, source_target_pairs={{0,24},{8,0},{16,8},{24,16},{32,56},{40,32},{48,40},{56,48},{64,88... | collective-permute-start | bytes 307208 | tf_op jit(solution)/shard_map/ppermute | solution.py:29
  219.8 5.8 %collective-permute-start.23 = (f32[8,3200]{1,0:T(8,128)S(1)}, f32[8,3200]{1,0:T(8,128)S(1)}, u32[]{:S(2)}, u32[]{:S(2)}) collective-permute-start(f32[8,3200]{1,0:T(8,128)S(1)} %get-tuple-element.65), channel_id=1, source_target_pairs={{0,8},{8,16},{16,24},{24,0},{32,40},{40,48},{48,56},{56,32},{64,72... | collective-permute-start | bytes 307208 | tf_op jit(solution)/shard_map/ppermute | solution.py:29
  242.7 2.5 collective-permute-start.37
  243.8 22.5 %collective-permute-start.46 = (f32[16,128]{1,0:T(8,128)S(1)}, f32[16,128]{1,0:T(8,128)S(1)}, u32[]{:S(2)}, u32[]{:S(2)}) collective-permute-start(f32[16,128]{1,0:T(8,128)S(1)} %get-tuple-element.34), channel_id=1, source_target_pairs={{0,4},{1,5},{2,6},{3,7},{4,0},{5,1},{6,2},{7,3},{8,12},{9,13},{10,... | collective-permute-start | bytes 24584 | tf_op jit(solution)/shard_map/ppermute | solution.py:29
  244.9 20.2 %collective-permute-start.45 = (f32[16,128]{1,0:T(8,128)S(1)}, f32[16,128]{1,0:T(8,128)S(1)}, u32[]{:S(2)}, u32[]{:S(2)}) collective-permute-start(f32[16,128]{1,0:T(8,128)S(1)} %get-tuple-element.34), channel_id=1, source_target_pairs={{0,2},{1,3},{2,4},{3,5},{4,6},{5,7},{6,0},{7,1},{8,10},{9,11},{10,... | collective-permute-start | bytes 24584 | tf_op jit(solution)/shard_map/ppermute | solution.py:29
  246.2 5.4 %collective-permute-start.38 = (f32[88,256]{1,0:T(8,128)S(1)}, f32[88,256]{1,0:T(8,128)S(1)}, u32[]{:S(2)}, u32[]{:S(2)}) collective-permute-start(f32[88,256]{1,0:T(8,128)S(1)} %get-tuple-element.68), channel_id=1, source_target_pairs={{0,4},{1,5},{2,6},{3,7},{4,0},{5,1},{6,2},{7,3},{8,12},{9,13},{10,... | collective-permute-start | bytes 270344 | tf_op jit(solution)/shard_map/ppermute | solution.py:29
  248.1 16.8 %collective-permute-start.40 = (f32[88,256]{1,0:T(8,128)S(1)}, f32[88,256]{1,0:T(8,128)S(1)}, u32[]{:S(2)}, u32[]{:S(2)}) collective-permute-start(f32[88,256]{1,0:T(8,128)S(1)} %get-tuple-element.69), channel_id=1, source_target_pairs={{0,6},{1,7},{2,0},{3,1},{4,2},{5,3},{6,4},{7,5},{8,14},{9,15},{10,... | collective-permute-start | bytes 270344 | tf_op jit(solution)/shard_map/ppermute | solution.py:29
  250.0 14.9 %collective-permute-start.39 = (f32[88,256]{1,0:T(8,128)S(1)}, f32[88,256]{1,0:T(8,128)S(1)}, u32[]{:S(2)}, u32[]{:S(2)}) collective-permute-start(f32[88,256]{1,0:T(8,128)S(1)} %get-tuple-element.70), channel_id=1, source_target_pairs={{0,2},{1,3},{2,4},{3,5},{4,6},{5,7},{6,0},{7,1},{8,10},{9,11},{10,... | collective-permute-start | bytes 270344 | tf_op jit(solution)/shard_map/ppermute | solution.py:29
  251.7 24.3 %collective-permute-start.47 = (f32[16,128]{1,0:T(8,128)S(1)}, f32[16,128]{1,0:T(8,128)S(1)}, u32[]{:S(2)}, u32[]{:S(2)}) collective-permute-start(f32[16,128]{1,0:T(8,128)S(1)} %get-tuple-element.34), channel_id=1, source_target_pairs={{0,6},{1,7},{2,0},{3,1},{4,2},{5,3},{6,4},{7,5},{8,14},{9,15},{10,... | collective-permute-start | bytes 24584 | tf_op jit(solution)/shard_map/ppermute | solution.py:29
  265.0 6.9 %collective-permute-start.41 = (f32[128,256]{1,0:T(8,128)S(1)}, f32[128,256]{1,0:T(8,128)S(1)}, u32[]{:S(2)}, u32[]{:S(2)}) collective-permute-start(f32[128,256]{1,0:T(8,128)S(1)} %get-tuple-element.71), channel_id=1, source_target_pairs={{0,2},{1,3},{2,4},{3,5},{4,6},{5,7},{6,0},{7,1},{8,10},{9,11},{10,... | collective-permute-start | bytes 393224 | tf_op jit(solution)/shard_map/ppermute | solution.py:29
  265.1 6.8 %collective-permute-start.42 = (f32[128,256]{1,0:T(8,128)S(1)}, f32[128,256]{1,0:T(8,128)S(1)}, u32[]{:S(2)}, u32[]{:S(2)}) collective-permute-start(f32[128,256]{1,0:T(8,128)S(1)} %get-tuple-element.71), channel_id=1, source_target_pairs={{0,4},{1,5},{2,6},{3,7},{4,0},{5,1},{6,2},{7,3},{8,12},{9,13},{10,... | collective-permute-start | bytes 393224 | tf_op jit(solution)/shard_map/ppermute | solution.py:29
  266.3 6.2 %collective-permute-start.43 = (f32[128,256]{1,0:T(8,128)S(1)}, f32[128,256]{1,0:T(8,128)S(1)}, u32[]{:S(2)}, u32[]{:S(2)}) collective-permute-start(f32[128,256]{1,0:T(8,128)S(1)} %get-tuple-element.71), channel_id=1, source_target_pairs={{0,6},{1,7},{2,0},{3,1},{4,2},{5,3},{6,4},{7,5},{8,14},{9,15},{10,... | collective-permute-start | bytes 393224 | tf_op jit(solution)/shard_map/ppermute | solution.py:29
  272.6 11.8 %collective-permute-start.44 = (f32[512,256]{1,0:T(8,128)S(1)}, f32[512,256]{1,0:T(8,128)S(1)}, u32[]{:S(2)}, u32[]{:S(2)}) collective-permute-start(f32[512,256]{1,0:T(8,128)S(1)} %constant_dynamic-update-slice_fusion.4), channel_id=1, source_target_pairs={{0,1},{1,0},{2,3},{3,2},{4,5},{5,4},{6,7},{7,6},{8,9},{9,8},{10,11... | collective-permute-start | bytes 1572872 | tf_op jit(solution)/shard_map/ppermute | solution.py:33
  275.9 1.6 collective-permute-start.48
  279.9 15.2 %all-to-all-start.2 = ((f32[16,32,256]{2,1,0:T(8,128)}), f32[16,32,256]{2,1,0:T(8,128)S(1)}, u32[]{:S(2)}, u32[]{:S(2)}) async-start(f32[16,32,256]{2,1,0:T(8,128)} %bitcast.15), calls=%async_computation.2 | async-start | bytes 1048576 | tf_op jit(solution)/shard_map/all_to_all | solution.py:554
  295.1 3.5 %copy-start.4 = (f32[16,32,256]{2,1,0:T(8,128)}, f32[16,32,256]{2,1,0:T(8,128)S(1)}, u32[]{:S(2)}) copy-start(f32[16,32,256]{2,1,0:T(8,128)S(1)} %all-to-all-done.2) | copy-start | bytes 1572868
  295.1 19.8 %all-to-all-start.1 = ((f32[16,16,256]{2,1,0:T(8,128)}), f32[16,16,256]{2,1,0:T(8,128)S(1)}, u32[]{:S(2)}, u32[]{:S(2)}) async-start(f32[16,16,256]{2,1,0:T(8,128)} %bitcast.17), calls=%async_computation.1 | async-start | bytes 524288 | tf_op jit(solution)/shard_map/all_to_all | solution.py:554
  (6 other events, 4.7 us)
Sparse Core Ops, SparseCore 0:
  176.9 56.1 all-gather.4
  235.2 45.9 all-gather.2
where the time goes:
time: 341 us; the launch traced here: 334 us
  waiting for transfers between devices  124 us (36%)
  starting transfers between devices  87.2 us (26%)
  Pallas kernels  82.8 us (24%)
  between operations  14.3 us (4%)
  local copies, waits for them, and re-layouts  14.1 us (4%)
  other arithmetic  11.9 us (3%)
    ppermute x42, waiting for transfers between devices, send(): lax.ppermute(value, 'tensor' if kind == 'x' else 'dp', ring(kind, step))  92.5 us
    ppermute x42, starting transfers between devices, send(): lax.ppermute(value, 'tensor' if kind == 'x' else 'dp', ring(kind, step))  55.8 us
    all_to_all x3, waiting for transfers between devices, hand_over_dp(): return lax.all_to_all(value, 'dp', 0, 0, tiled=True)  20.8 us
    pallas_call x1, Pallas kernels, factors(): call(functools.partial(factor_kernel, counts), [array(R, R), array(R, R),...  16.3 us
    all_to_all x3, starting transfers between devices, hand_over_dp(): return lax.all_to_all(value, 'dp', 0, 0, tiled=True)  15.8 us
    pallas_call x2, Pallas kernels, sketches(): call(sketch_kernel, [array(count, 2 * R), array(16, 128)], grid_spec=grid...  12.6 us
    pallas_call x1, Pallas kernels, last_update(): call(last_kernel, array(count, columns), grid=(columns // TILE,), in_spec...  11.7 us
    ppermute x6, starting transfers between devices, swap_cores(): return lax.ppermute(value, 'tensor', [(i, i ^ 1) for i in range(8)])  11.3 us
  transfers between devices with their start and end apart: 54, of which 26 were waited for; matrix products, arithmetic and copies ran while one was open for 5% of the time, Pallas kernels for 14%

commit v1 on v0

--- a/solution.py
+++ b/solution.py
@@ -12,7 +12,7 @@
 R = 256
 TILE = 512
 BLOCK = 64
-VMEM_LIMIT = 60 * 1024 * 1024
+VMEM_LIMIT = 48 * 1024 * 1024
 
 DAMPING = 0.1
 
@@ -65,37 +65,6 @@
 def scatter_dp(first, second):
     first, second = scatter_four(first, "y"), scatter_four(second, "z")
     return jnp.concatenate([scatter_four(first, "z"), scatter_four(second, "y")])
-
-
-def scatter_dp_after(first, second, after):
-    halves = []
-    for value, kind in ((first, "y"), (second, "z")):
-        here, count = place(kind), value.shape[0] // 4
-        parts = [
-            send(rows(value, (here + step) % 4, count), kind, step) for step in (2, 1, 3)
-        ]
-        halves.append(sum_blocks(here, value, parts, after))
-    return jnp.concatenate([scatter_four(halves[0], "z"), scatter_four(halves[1], "y")])
-
-
-def sum_kernel(here, value, two, one, three, after, out):
-    out[...] = (value[...] + two[...]) + (one[...] + three[...])
-
-
-def sum_blocks(here, value, parts, after):
-    count, columns = parts[0].shape
-    whole = pl.BlockSpec((count, columns), lambda i, h: (0, 0))
-    grid_spec = pltpu.PrefetchScalarGridSpec(
-        num_scalar_prefetch=1,
-        grid=(1,),
-        in_specs=[pl.BlockSpec((count, columns), lambda i, h: (h[0], 0))]
-        + [whole] * 3
-        + [pl.BlockSpec(memory_space=pl.ANY)],
-        out_specs=whole,
-    )
-    return call(sum_kernel, array(count, columns), grid_spec=grid_spec, name="sum_blocks")(
-        here.astype(jnp.int32).reshape(1), value, *parts, after
-    )
 
 
 def store_groups(first, second, columns, value):
@@ -218,188 +187,152 @@
     flipped[:, pl.ds(pl.multiple_of((1 - core) * half, 128), half)] = other[...].T
 
 
-def range_grad_kernel(
-    tokens_all, place_ref, own, other, grads, sq_one, sq_two, act, first, second, piece, flipped, rounded
+def ranges_kernel(
+    tokens_all, places, own, other, grads, acts, sq_one, sq_two, first, second, flipped, rounded, range_act
 ):
     step = pl.program_id(0)
     columns = grads.shape[1]
+    whole = pl.num_programs(0) * columns
 
     @pl.when(step == 0)
     def _():
-        flip_halves(place_ref[1], own, other, flipped)
+        half = own.shape[0]
+        flipped[:, pl.ds(pl.multiple_of(places[1] * half, 128), half)] = own[...].T
+        flipped[:, pl.ds(pl.multiple_of((1 - places[1]) * half, 128), half)] = other[...].T
         rounded[...] = flipped[...].astype(jnp.bfloat16)
-        total = act[0:48, :]
-        for d in range(1, 16):
-            total += act[48 * d : 48 * d + 48, :]
-        piece[...] = total
-
-    part = jnp.dot(rounded[...], grads[...], preferred_element_type=jnp.float32)
+
+    part = jnp.dot(rounded[:R, :], grads[...], preferred_element_type=jnp.float32)
     to = pl.ds(pl.multiple_of(step * columns, 128), columns)
     store_groups(first, second, to, part / tokens_all)
 
     @pl.when(step == pl.num_programs(0) - 1)
     def _():
-        some = flipped[pl.ds(pl.multiple_of(place_ref[0] * 32, 32), 32), :]
-        core = product(split(flipped[...]), split(some), LAST) / tokens_all
-        lane = lax.broadcasted_iota(jnp.int32, (R, 96), 1)
+        cores = []
+        for low in (0, R):
+            some = flipped[pl.ds(pl.multiple_of(low + places[0] * 32, 32), 32), :]
+            core = product(split(flipped[low : low + R, :]), split(some), LAST)
+            cores.append(core / tokens_all)
+        lane = lax.broadcasted_iota(jnp.int32, (R, 64), 1)
         squares = sq_one[...] + sq_two[...]
         traces = jnp.where(lane == 0, squares[0:1, 0:1], 0.0)
         traces = jnp.where(lane == 1, squares[8:9, 0:1], traces)
-        rest = jnp.concatenate([core, traces], axis=1)
-        store_groups(first, second, pl.ds(first.shape[1] - 128, 128), rest)
-
-
-def range_grad_of(places, own, other, grads, sq_one, sq_two, act, tokens_all):
+        rest = jnp.concatenate(cores + [traces], axis=1)
+        store_groups(first, second, pl.ds(whole, 128), rest)
+        part = jnp.dot(rounded[R:, :], acts[...], preferred_element_type=jnp.float32)
+        range_act[...] = part.T / tokens_all
+        for d in range(16):
+            for i in range(3):
+                to = pl.ds(whole + 128 + i * R, R)
+                at, here = d % 4 * 4 + d // 4, 48 * d + 16 * i
+                first[8 * at : 8 * at + 8, to] = range_act[here : here + 8, :]
+                second[8 * d : 8 * d + 8, to] = range_act[here + 8 : here + 16, :]
+
+
+def ranges(places, own, other, grads, acts, sq_one, sq_two, tokens_all):
     count, columns = grads.shape
-    whole = lambda shape: pl.BlockSpec(shape, lambda j, c: (0, 0))
+    fixed = lambda shape: pl.BlockSpec(shape, lambda j, c: (0, 0))
+    total = columns + 128 + 3 * R
     grid_spec = pltpu.PrefetchScalarGridSpec(
         num_scalar_prefetch=1,
         grid=(columns // TILE,),
         in_specs=[
-            whole((count // 2, R)),
-            whole((count // 2, R)),
+            fixed(own.shape),
+            fixed(other.shape),
             pl.BlockSpec((count, TILE), lambda j, c: (0, j)),
-            whole((16, 128)),
-            whole((16, 128)),
-            whole((768, R)),
-        ],
-        out_specs=[whole((R // 2, columns + 128))] * 2 + [whole((48, R))],
+            fixed(acts.shape),
+            fixed((16, 128)),
+            fixed((16, 128)),
+        ],
+        out_specs=[fixed((R // 2, total))] * 2,
         scratch_shapes=[
-            pltpu.VMEM((R, count), jnp.float32),
-            pltpu.VMEM((R, count), jnp.bfloat16),
+            pltpu.VMEM((2 * R, count), jnp.float32),
+            pltpu.VMEM((2 * R, count), jnp.bfloat16),
+            pltpu.VMEM((acts.shape[1], R), jnp.float32),
         ],
     )
     return call(
-        functools.partial(range_grad_kernel, tokens_all),
-        [array(R // 2, columns + 128)] * 2 + [array(48, R)],
+        functools.partial(ranges_kernel, tokens_all),
+        [array(R // 2, total)] * 2,
         grid_spec=grid_spec,
-        name="range_grad",
-    )(places, own, other, grads, sq_one, sq_two, act)
-
-
-def range_act_kernel(tokens_all, place_ref, own, other, acts, out, core, flipped):
-    flip_halves(place_ref[1], own, other, flipped)
-    part = jnp.dot(
-        flipped[...].astype(jnp.bfloat16), acts[...], preferred_element_type=jnp.float32
-    )
-    out[...] = part.T / tokens_all
-    some = flipped[pl.ds(pl.multiple_of(place_ref[0] * 32, 32), 32), :]
-    core[:, :32] = product(split(flipped[...]), split(some), LAST) / tokens_all
-    core[:, 32:] = jnp.zeros((R, 96), jnp.float32)
-
-
-def range_act_of(places, own, other, acts, tokens_all):
-    count, columns = acts.shape
-    whole = lambda shape, j=0: pl.BlockSpec(shape, lambda i, c: (0, j))
-    grid_spec = pltpu.PrefetchScalarGridSpec(
-        num_scalar_prefetch=1,
-        grid=(1,),
-        in_specs=[whole((count // 2, R), 1), whole((count // 2, R), 1), whole((count, columns))],
-        out_specs=[whole((columns, R)), whole((R, 128))],
-        scratch_shapes=[pltpu.VMEM((R, count), jnp.float32)],
-    )
-    return call(
-        functools.partial(range_act_kernel, tokens_all),
-        [array(columns, R), array(R, 128)],
-        grid_spec=grid_spec,
-        name="range_act",
-    )(places, own, other, acts)
-
-
-def left_kernel(place_ref, rows_act, core, weight, first, second, flipped, high, low):
+        name="ranges",
+    )(places, own, other, grads, acts, sq_one, sq_two)
+
+
+def left_kernel(rows_act, weight, first, second, high, low):
     step = pl.program_id(0)
     columns = weight.shape[1]
 
     @pl.when(step == 0)
     def _():
-        flipped[...] = rows_act[...].T
-        high[...], low[...] = split(flipped[...])
-        some = flipped[pl.ds(pl.multiple_of(place_ref[0] * 32, 32), 32), :]
-        gram = product((high[...], low[...]), split(some), LAST)
-        rest = jnp.concatenate([gram, core[:, :96]], axis=1)
-        store_groups(first, second, pl.ds(first.shape[1] - 128, 128), rest)
+        high[...], low[...] = split(rows_act[...].T)
 
     part = product((high[...], low[...]), split(weight[...]), INNER)
     store_groups(first, second, pl.ds(pl.multiple_of(step * columns, 128), columns), part)
 
 
-def left_products(places, rows_act, core, weight):
+def left_products(rows_act, weight):
     count, columns = weight.shape
-    whole = lambda shape: pl.BlockSpec(shape, lambda j, c: (0, 0))
-    grid_spec = pltpu.PrefetchScalarGridSpec(
-        num_scalar_prefetch=1,
+    return call(
+        left_kernel,
+        [array(R // 2, columns)] * 2,
         grid=(columns // TILE,),
         in_specs=[
-            whole((count, R)),
-            whole((R, 128)),
-            pl.BlockSpec((count, TILE), lambda j, c: (0, j)),
-        ],
-        out_specs=[whole((R // 2, columns + 128))] * 2,
-        scratch_shapes=[
-            pltpu.VMEM((R, count), jnp.float32),
-            pltpu.VMEM((R, count), jnp.bfloat16),
-            pltpu.VMEM((R, count), jnp.bfloat16),
-        ],
-    )
-    return call(
-        left_kernel,
-        [array(R // 2, columns + 128)] * 2,
-        grid_spec=grid_spec,
+            pl.BlockSpec((count, R), lambda j: (0, 0)),
+            pl.BlockSpec((count, TILE), lambda j: (0, j)),
+        ],
+        out_specs=[pl.BlockSpec((R // 2, columns), lambda j: (0, 0))] * 2,
+        scratch_shapes=[pltpu.VMEM((R, count), jnp.bfloat16)] * 2,
         name="left_products",
-    )(places, rows_act, core, weight)
-
-
-def right_kernel(whole, weight, left, sums):
+    )(rows_act, weight)
+
+
+def right_kernel(whole, one, two, three, weight, left, sums):
     @pl.when(pl.program_id(0) == 0)
     def _():
         sums[...] = jnp.zeros_like(sums)
+        pieces = split(jnp.concatenate([one[...], two[...], three[...]]))
+        gram = product(pieces, pieces, ((0,), (0,)))
+        for i in range(8):
+            sums[i * 120 + 80 : i * 120 + 112, :] = gram[i * 32 : i * 32 + 32]
 
     ranges = split(whole[...])
     right = product(split(weight[...]), ranges, LAST)
     gram = product(ranges, ranges, LAST)
     both = product(split(left[...]), ranges, LAST)
     for i in range(8):
-        at = i * 88
+        at = i * 120
         sums[at : at + 48, :] += right[i * 48 : i * 48 + 48]
         sums[at + 48 : at + 80, :] += gram[i * 32 : i * 32 + 32]
-        sums[at + 80 : at + 82, :] += both[i * 2 : i * 2 + 2]
-
-
-def right_products(whole, weight, left):
+        sums[at + 112 : at + 114, :] += both[i * 2 : i * 2 + 2]
+
+
+def right_products(whole, extra, weight, left):
     count, columns = weight.shape
     return call(
         right_kernel,
-        array(704, R),
+        array(960, R),
         grid=(columns // TILE,),
-        in_specs=[
-            pl.BlockSpec((R, TILE), lambda j: (0, j)),
+        in_specs=[pl.BlockSpec((R, TILE), lambda j: (0, j))]
+        + [pl.BlockSpec((R, R), lambda j: (0, 0))] * 3
+        + [
             pl.BlockSpec((count, TILE), lambda j: (0, j)),
             pl.BlockSpec((16, TILE), lambda j: (0, j)),
         ],
-        out_specs=pl.BlockSpec((704, R), lambda j: (0, 0)),
+        out_specs=pl.BlockSpec((960, R), lambda j: (0, 0)),
         name="right_products",
-    )(whole, weight, left)
-
-
-def pack_small_kernel(parts, out):
-    parts = [parts[i * 16 : i * 16 + 16, :] for i in range(8)]
-    gram = jnp.concatenate([p[:, :32] for p in parts], axis=1)
-    core = jnp.concatenate([p[:, 32:64] for p in parts], axis=1)
-    for d in range(16):
-        out[32 * d : 32 * d + 16, :] = gram
-        out[32 * d + 16 : 32 * d + 32, :] = core
-
-
-def pack_both_kernel(right, out):
+    )(whole, *extra, weight, left)
+
+
+def pack_kernel(right, out):
     for d in range(16):
         for i in range(8):
             at = 16 * d + 2 * i
-            out[at : at + 2, :] = right[i * 128 + 80 : i * 128 + 82, :]
-
-
-def pack(kernel, value, count, name):
+            out[at : at + 2, :] = right[i * 192 + 112 : i * 192 + 114, :]
+
+
+def pack(right):
     whole = pl.BlockSpec(memory_space=pltpu.VMEM)
-    return call(kernel, array(count, R), in_specs=[whole], out_specs=whole, name=name)(value)
+    return call(pack_kernel, array(R, R), in_specs=[whole], out_specs=whole, name="pack")(right)
 
 
 def exact(left, right, dims):
@@ -472,12 +405,12 @@
                 w[high:, :] -= exact(line[:, high:R], line, ((0,), (0,)))
 
 
-def factor_kernel(counts, right, small, inverse_act, inverse_grad, scale, *work):
+def factor_kernel(counts, right, inverse_act, inverse_grad, scale, *work):
     trace_grad, trace_act = jnp.zeros((1, 1)), jnp.zeros((1, 1))
     for i in range(8):
-        at = i * 128 + 120
-        trace_grad += right[at : at + 1, 32:33]
-        trace_act += right[at : at + 1, 33:34]
+        at = i * 192 + 184
+        trace_grad += right[at : at + 1, 64:65]
+        trace_act += right[at : at + 1, 65:66]
     damp_grad = DAMPING * trace_grad / counts[0]
     damp_act = DAMPING * trace_act / counts[1]
     scale[...] = jnp.broadcast_to(1.0 / (damp_act * damp_grad), (8, 128))
@@ -487,24 +420,22 @@
     for w in work:
         w[:, R:] = identity
     for i in range(8):
-        at, here = slice(i * 32, i * 32 + 32), i * 128
-        work[1][at, :R] = damp_grad * right[here + 88 : here + 120, :] + right[here + 48 : here + 80, :]
-    for d in range(16):
-        at, here = slice(d * 16, d * 16 + 16), d * 32
-        work[0][at, :R] = damp_act * small[here + 16 : here + 32, :] + small[here : here + 16, :]
+        at, here = slice(i * 32, i * 32 + 32), i * 192
+        work[0][at, :R] = damp_act * right[here + 152 : here + 184, :] + right[here + 80 : here + 112, :]
+        work[1][at, :R] = damp_grad * right[here + 120 : here + 152, :] + right[here + 48 : here + 80, :]
     lower_inverses(work, (inverse_act, inverse_grad))
 
 
-def factors(right, small, counts):
+def factors(right, counts):
     whole = pl.BlockSpec(memory_space=pltpu.VMEM)
     return call(
         functools.partial(factor_kernel, counts),
         [array(R, R), array(R, R), array(8, 128)],
-        in_specs=[whole] * 2,
+        in_specs=[whole],
         out_specs=[whole] * 3,
         scratch_shapes=[pltpu.VMEM((R, 2 * R), jnp.float32)] * 2,
         name="factors",
-    )(right, small)
+    )(right)
 
 
 def applied(value, inverse):
@@ -519,7 +450,7 @@
     @pl.when(pl.program_id(0) == 0)
     def _():
         for i in range(8):
-            sums[i * 48 : i * 48 + 48, :] = right[i * 128 : i * 128 + 48, :]
+            sums[i * 48 : i * 48 + 48, :] = right[i * 192 : i * 192 + 48, :]
         solved = applied(rows_act[...], inverse_act[...])
         pieces[0][...], pieces[1][...] = split(solved)
         rest = sums[...] - product(split(solved), split(both[...]), INNER)
@@ -567,38 +498,35 @@
     own = gather_four(scatter_four(part + other, "x"), "x")
     other = swap_cores(own)
 
-    part, core = range_act_of(places, own, other, acts, tokens_all)
-    part = hand_over_dp(part)
-    first, second, piece = range_grad_of(
-        places, own, other, grads_out, sq_one, sq_two, part, tokens_all
-    )
-
+    piece = scatter_dp(
+        *ranges(places, own, other, grads_out, acts, sq_one, sq_two, tokens_all)
+    )
+    gathered = lax.all_gather(piece, "dp", axis=0, tiled=True)
+
+    at = columns + 128
+    piece = jnp.concatenate([piece[:, at + i * R : at + i * R + R] for i in range(3)])
     moves = []
     for d in range(16):
         for t in range(8):
             k = d % 8
             moves.append((d * 8 + t, (2 * t + d // 8) * 8 + 2 * (k % 4) + k // 4))
-    piece = lax.ppermute(piece, ("dp", "tensor"), moves)
-    rows_act = gather_tensor(piece)
-
-    piece = scatter_dp_after(first, second, rows_act)
-    range_grad = lax.all_gather(piece, "dp", axis=0, tiled=True)
-
-    piece = scatter_dp(*left_products(places, rows_act, core, weight_grad))
+    rows_act = gather_tensor(lax.ppermute(piece, ("dp", "tensor"), moves))
+
+    piece = scatter_dp(*left_products(rows_act, weight_grad))
     left_sums = lax.all_gather(piece, "dp", axis=0, tiled=True)
-    small = gather_tensor(piece[:, columns:])
-    small = hand_over_dp(pack(pack_small_kernel, small, 512, "pack_small"))
-
-    part = scatter_tensor(right_products(range_grad, weight_grad, piece))
-    extra = range_grad[:, columns:]
+
+    blocks = [gathered[:, at + i * R : at + i * R + R] for i in range(3)]
+    part = scatter_tensor(right_products(gathered, blocks, weight_grad, piece))
+    extra = gathered[:, columns:at]
+    cores = extra[:, : 2 * width].T
     rest = jnp.pad(extra[:8], ((0, 0), (0, R - 128)))
-    right = gather_tensor(jnp.concatenate([part, extra[:, :width].T, rest]))
-    both = hand_over_dp(pack(pack_both_kernel, right, R, "pack_both"))
+    right = gather_tensor(jnp.concatenate([part, cores, rest]))
+    both = lax.all_to_all(pack(right), "dp", 0, 0, tiled=True)
 
     counts = (float(tokens_all * FF), float(tokens_all * D))
-    inverse_act, inverse_grad, scale = factors(right, small, counts)
+    inverse_act, inverse_grad, scale = factors(right, counts)
     return last_update(
-        left_sums, weight_grad, range_grad, right, both, rows_act, inverse_act, inverse_grad, scale
+        left_sums, weight_grad, gathered, right, both, rows_act, inverse_act, inverse_grad, scale
     )
 
 

time: 341 us -> 307 us (0.900)
  Pallas kernels: 82.8 us -> 62 us
  waiting for transfers between devices: 124 us -> 107 us
  starting transfers between devices: 87.2 us -> 93.6 us
  other arithmetic: 11.9 us -> 6.86 us
  local copies, waits for them, and re-layouts: 14.1 us -> 18.5 us
    all_to_all x3 -> x1, waiting for transfers between devices: 20.8 us -> 0.01 us  [body(): both = lax.all_to_all(pack(right), 'dp', 0, 0, tiled=True)]
    ppermute x42 -> x39, starting transfers between devices: 55.8 us -> 71.3 us  [send(): lax.ppermute(value, 'tensor' if kind == 'x' else 'dp', ring(kind, step))]
    pallas_call x8 -> x4, Pallas kernels: 42.3 us -> 27 us  [the longest x1 12.5 us: ranges(): call(functools.partial(ranges_kernel, tokens_all), [array(R // 2, total)]...]
    all_to_all x3 -> x1, starting transfers between devices: 15.8 us -> 3.53 us  [body(): both = lax.all_to_all(pack(right), 'dp', 0, 0, tiled=True)]
    unnamed x32 -> x30, local copies, waits for them, and re-layouts: 5.8 us -> 13.4 us
    all_gather x1, waiting for transfers between devices: 6.79 us -> 0.02 us  [body(): gathered = lax.all_gather(piece, 'dp', axis=0, tiled=True)]
    ppermute x42 -> x39, waiting for transfers between devices: 92.5 us -> 97.8 us  [send(): lax.ppermute(value, 'tensor' if kind == 'x' else 'dp', ring(kind, step))]
    dynamic_slice x11, local copies, waits for them, and re-layouts: 6.2 us -> 1.79 us  [rows(): return lax.dynamic_slice_in_dim(value, index * count, count, 0)]
  transfers between devices with their start and end apart: 54 -> 48, of which waited for: 26 -> 29; matrix products, arithmetic and copies ran while one was open for 5% -> 2% of each run, Pallas kernels for 14% -> 11%
where the time goes in v1:
time: 307 us; the launch traced here: 302 us
  waiting for transfers between devices  107 us (35%)
  starting transfers between devices  93.6 us (30%)
  Pallas kernels  62 us (20%)
  local copies, waits for them, and re-layouts  18.5 us (6%)
  between operations  14.1 us (5%)
  other arithmetic  6.86 us (2%)
    ppermute x39, waiting for transfers between devices, send(): lax.ppermute(value, 'tensor' if kind == 'x' else 'dp', ring(kind, step))  97.8 us
    ppermute x39, starting transfers between devices, send(): lax.ppermute(value, 'tensor' if kind == 'x' else 'dp', ring(kind, step))  71.3 us
    pallas_call x1, Pallas kernels, factors(): call(functools.partial(factor_kernel, counts), [array(R, R), array(R, R),...  14.1 us
    unnamed x30, local copies, waits for them, and re-layouts  13.4 us
    ppermute x5, starting transfers between devices, swap_cores(): return lax.ppermute(value, 'tensor', [(i, i ^ 1) for i in range(8)])  13.3 us
    pallas_call x1, Pallas kernels, ranges(): call(functools.partial(ranges_kernel, tokens_all), [array(R // 2, total)]...  12.5 us
    pallas_call x1, Pallas kernels, last_update(): call(last_kernel, array(count, columns), grid=(columns // TILE,), in_spec...  10.5 us
    pallas_call x2, Pallas kernels, sketches(): call(sketch_kernel, [array(count, 2 * R), array(16, 128)], grid_spec=grid...  10.4 us
  transfers between devices with their start and end apart: 48, of which 29 were waited for; matrix products, arithmetic and copies ran while one was open for 2% of the time, Pallas kernels for 11%

profile of v1, /device:TPU:1, one launch (start us, length us, event | category | flops | bytes accessed | tf_op | source)
XLA Modules:
  0.0 301.8 jit_solution(9632045135628656094)
XLA Ops:
  6.5 1.7 copy-done
  8.2 1.4 copy-done.3
  10.6 5.7 %sketches.3 = (f32[768,512]{1,0:T(8,128)}, f32[16,128]{1,0:T(8,128)S(1)}) custom-call(s32[1]{0:T(128)} %bitcast.2.core, bf16[1536,3072]{1,0:T(8,128)(2,1)} %grads.5, bf16[1536,768]{1,0:T(8,128)(2,1)S(1)} %copy-done, bf16[3072,256]{1,0:T(8,128)(2,1)S(1)} %copy-done.3, bf16[768,256]{1,0:T(8,128)(2,1)S(1)} %copy-done.8), custom_call_target="tpu_custom_call" | custom-call | tf_op jit(solution)/shard_map/sketches/pallas_call | solution.py:172
  16.3 1.4 collective-permute-start
  17.8 1.4 copy-done.4
  19.2 4.7 %sketches.2 = (f32[768,512]{1,0:T(8,128)S(1)}, f32[16,128]{1,0:T(8,128)S(1)}) custom-call(s32[1]{0:T(128)} %bitcast.1.core, bf16[1536,3072]{1,0:T(8,128)(2,1)} %grads.5, bf16[1536,768]{1,0:T(8,128)(2,1)S(1)} %copy-done.1, bf16[3072,256]{1,0:T(8,128)(2,1)S(1)} %copy-done.4, bf16[768,256]{1,0:T(8,128)(2,1)S(1)} %copy-done.9), custom_call_target="tpu_custom_call" | custom-call | tf_op jit(solution)/shard_map/sketches/pallas_call | solution.py:172
  23.9 1.1 copy-done.10
  25.0 2.2 add.360
  27.3 2.9 collective-permute-start.1
  31.7 8.0 %collective-permute-done.1 = f32[192,512]{1,0:T(8,128)S(1)} collective-permute-done((f32[192,512]{1,0:T(8,128)S(1)}, f32[192,512]{1,0:T(8,128)S(1)}, u32[]{:S(2)}, u32[]{:S(2)}) %collective-permute-start.1) | collective-permute-done | bytes 393248 | tf_op jit(solution)/shard_map/ppermute | solution.py:29
  39.7 8.7 %collective-permute-done.3 = f32[192,512]{1,0:T(8,128)S(1)} collective-permute-done((f32[192,512]{1,0:T(8,128)S(1)}, f32[192,512]{1,0:T(8,128)S(1)}, u32[]{:S(2)}, u32[]{:S(2)}) %collective-permute-start.3) | collective-permute-done | bytes 393248 | tf_op jit(solution)/shard_map/ppermute | solution.py:29
  50.2 1.3 constant_dynamic-update-slice_fusion.11
  51.4 1.5 collective-permute-start.4
  52.9 2.3 collective-permute-start.5
  55.7 6.9 %collective-permute-done.4 = f32[192,512]{1,0:T(8,128)S(1)} collective-permute-done((f32[192,512]{1,0:T(8,128)S(1)}, f32[192,512]{1,0:T(8,128)S(1)}, u32[]{:S(2)}, u32[]{:S(2)}) %collective-permute-start.4) | collective-permute-done | bytes 393248 | tf_op jit(solution)/shard_map/ppermute | solution.py:29
  62.7 9.7 %collective-permute-done.5 = f32[192,512]{1,0:T(8,128)S(1)} collective-permute-done((f32[192,512]{1,0:T(8,128)S(1)}, f32[192,512]{1,0:T(8,128)S(1)}, u32[]{:S(2)}, u32[]{:S(2)}) %collective-permute-start.5) | collective-permute-done | bytes 393248 | tf_op jit(solution)/shard_map/ppermute | solution.py:29
  72.5 1.4 collective-permute-start.7
  74.0 3.0 collective-permute-done.7.other
  76.9 12.5 %ranges.1 = (f32[128,3968]{1,0:T(8,128)S(1)}, f32[128,3968]{1,0:T(8,128)}) custom-call(s32[2]{0:T(128)S(1)} %pad_add_fusion.places, f32[768,512]{1,0:T(8,128)S(1)} %constant_dynamic-update-slice_fusion.8.own, f32[768,512]{1,0:T(8,128)S(1)} %collective-permute-done.7.other, bf16[1536,3072]{1,0:T(8,128)(2,1)} %grads.5, bf16[1536,768]{1,0:T(8,128)(2,1)} %acts.5, ...), custom_call_target="tpu_custom_call" | custom-call | tf_op jit(solution)/shard_map/ranges/pallas_call | solution.py:253
  89.5 1.3 copy-done.6
  90.8 1.2 constant_dynamic-slice_fusion.27
  92.0 2.9 collective-permute-start.8
  96.4 3.7 %collective-permute-start.14 = (f32[32,3968]{1,0:T(8,128)S(1)}, f32[32,3968]{1,0:T(8,128)S(1)}, u32[]{:S(2)}, u32[]{:S(2)}) collective-permute-start(f32[32,3968]{1,0:T(8,128)S(1)} %get-tuple-element.32), channel_id=1, source_target_pairs={{0,64},{8,72},{16,80},{24,88},{32,96},{40,104},{48,112},{56,120},{... | collective-permute-start | bytes 1523720 | tf_op jit(solution)/shard_map/ppermute | solution.py:29
  100.6 5.9 %collective-permute-done.8 = f32[32,3968]{1,0:T(8,128)S(1)} collective-permute-done((f32[32,3968]{1,0:T(8,128)}, f32[32,3968]{1,0:T(8,128)S(1)}, u32[]{:S(2)}, u32[]{:S(2)}) %collective-permute-start.8) | collective-permute-done | bytes 507936 | tf_op jit(solution)/shard_map/ppermute | solution.py:29
  106.5 1.6 collective-permute-start.15
  108.1 9.6 %collective-permute-done.10 = f32[32,3968]{1,0:T(8,128)S(1)} collective-permute-done((f32[32,3968]{1,0:T(8,128)}, f32[32,3968]{1,0:T(8,128)S(1)}, u32[]{:S(2)}, u32[]{:S(2)}) %collective-permute-start.10) | collective-permute-done | bytes 507936 | tf_op jit(solution)/shard_map/ppermute | solution.py:29
  119.2 3.7 %collective-permute-start.11 = (f32[8,3968]{1,0:T(8,128)S(1)}, f32[8,3968]{1,0:T(8,128)S(1)}, u32[]{:S(2)}, u32[]{:S(2)}) collective-permute-start(f32[8,3968]{1,0:T(8,128)S(1)} %get-tuple-element.52), channel_id=1, source_target_pairs={{0,64},{8,72},{16,80},{24,88},{32,96},{40,104},{48,112},{56,120},{... | collective-permute-start | bytes 380936 | tf_op jit(solution)/shard_map/ppermute | solution.py:29
  124.8 3.0 collective-permute-start.17
  130.1 2.9 collective-permute-done.19
  133.0 1.2 collective-permute-done.18
  135.0 5.4 %collective-permute-start.20 = (f32[48,256]{1,0:T(8,128)S(1)}, f32[48,256]{1,0:T(8,128)S(1)}, u32[]{:S(2)}, u32[]{:S(2)}) collective-permute-start(f32[48,256]{1,0:T(8,128)S(1)} %pad_maximum_fusion.4), channel_id=1, source_target_pairs={{0,0},{1,16},{2,32},{3,48},{4,64},{5,80},{6,96},{7,112},{8,2},{9,1... | collective-permute-start | bytes 147464 | tf_op jit(solution)/shard_map/ppermute | solution.py:513
  140.5 1.4 collective-permute-done.20
  141.9 5.2 %collective-permute-start.23 = (f32[48,256]{1,0:T(8,128)S(1)}, f32[48,256]{1,0:T(8,128)S(1)}, u32[]{:S(2)}, u32[]{:S(2)}) collective-permute-start(f32[48,256]{1,0:T(8,128)S(1)} %collective-permute-done.20), channel_id=1, source_target_pairs={{0,6},{1,7},{2,0},{3,1},{4,2},{5,3},{6,4},{7,5},{8,14},{9,15},{10,... | collective-permute-start | bytes 147464 | tf_op jit(solution)/shard_map/ppermute | solution.py:29
  147.8 4.3 %collective-permute-done.21 = f32[48,256]{1,0:T(8,128)S(1)} collective-permute-done((f32[48,256]{1,0:T(8,128)S(1)}, f32[48,256]{1,0:T(8,128)S(1)}, u32[]{:S(2)}, u32[]{:S(2)}) %collective-permute-start.21) | collective-permute-done | bytes 49184 | tf_op jit(solution)/shard_map/ppermute | solution.py:29
  152.2 3.0 %collective-permute-start.24 = (f32[192,256]{1,0:T(8,128)S(1)}, f32[192,256]{1,0:T(8,128)S(1)}, u32[]{:S(2)}, u32[]{:S(2)}) collective-permute-start(f32[192,256]{1,0:T(8,128)S(1)} %constant_dynamic-update-slice_fusion.4), channel_id=1, source_target_pairs={{0,1},{1,0},{2,3},{3,2},{4,5},{5,4},{6,7},{7,6},{8,9},{9,8},{10,11... | collective-permute-start | bytes 589832 | tf_op jit(solution)/shard_map/ppermute | solution.py:33
  156.4 5.8 %left_products.1 = (f32[128,3072]{1,0:T(8,128)S(1)}, f32[128,3072]{1,0:T(8,128)S(1)}) custom-call(f32[384,256]{1,0:T(8,128)S(1)} %pad_maximum_fusion.2.rows_act, f32[384,3072]{1,0:T(8,128)} %weight.5), custom_call_target="tpu_custom_call" | custom-call | tf_op jit(solution)/shard_map/left_products/pallas_call | solution.py:275
  162.4 4.9 %collective-permute-start.27 = (f32[32,3072]{1,0:T(8,128)S(1)}, f32[32,3072]{1,0:T(8,128)S(1)}, u32[]{:S(2)}, u32[]{:S(2)}) collective-permute-start(f32[32,3072]{1,0:T(8,128)S(1)} %get-tuple-element.41), channel_id=1, source_target_pairs={{0,24},{8,0},{16,8},{24,16},{32,56},{40,32},{48,40},{56,48},{64,88... | collective-permute-start | bytes 1179656 | tf_op jit(solution)/shard_map/ppermute | solution.py:29
  167.5 2.1 collective-permute-start.33
  169.5 9.6 %collective-permute-done.25 = f32[32,3072]{1,0:T(8,128)S(1)} collective-permute-done((f32[32,3072]{1,0:T(8,128)S(1)}, f32[32,3072]{1,0:T(8,128)S(1)}, u32[]{:S(2)}, u32[]{:S(2)}) %collective-permute-start.25) | collective-permute-done | bytes 393248 | tf_op jit(solution)/shard_map/ppermute | solution.py:29
  179.1 2.0 collective-permute-start.32
  181.1 12.8 %collective-permute-done.27 = f32[32,3072]{1,0:T(8,128)S(1)} collective-permute-done((f32[32,3072]{1,0:T(8,128)S(1)}, f32[32,3072]{1,0:T(8,128)S(1)}, u32[]{:S(2)}, u32[]{:S(2)}) %collective-permute-start.27) | collective-permute-done | bytes 393248 | tf_op jit(solution)/shard_map/ppermute | solution.py:29
  195.0 3.3 %collective-permute-start.30 = (f32[8,3072]{1,0:T(8,128)S(1)}, f32[8,3072]{1,0:T(8,128)S(1)}, u32[]{:S(2)}, u32[]{:S(2)}) collective-permute-start(f32[8,3072]{1,0:T(8,128)S(1)} %get-tuple-element.59), channel_id=1, source_target_pairs={{0,96},{8,104},{16,112},{24,120},{32,0},{40,8},{48,16},{56,24},{64... | collective-permute-start | bytes 294920 | tf_op jit(solution)/shard_map/ppermute | solution.py:29
  199.9 1.6 collective-permute-done.32
  201.6 2.9 collective-permute-start.34
  206.7 2.0 collective-permute-done.36
  208.6 1.5 collective-permute-done.35
  210.9 1.2 fusion.3
  212.2 2.1 copy-done.2
  214.3 7.8 %right_products.1 = f32[960,256]{1,0:T(8,128)S(1)} custom-call(f32[256,3968]{1,0:T(8,128)S(1)} %copy-done.2, f32[256,256]{1,0:T(8,128)S(1)} %get-tuple-element.31.one, f32[256,256]{1,0:T(8,128)S(1)} %get-tuple-element.30.two, f32[256,256]{1,0:T(8,128)S(1)} %get-tuple-element.29.three, f32[384,3072]{1,0:T(8,128)} %weight.5, f32[16,3072]{1,0:T(8,128)S(1)} %copy-done.7), custom_call_target="tpu_custom_call" | custom-call | tf_op jit(solution)/shard_map/right_products/pallas_call | solution.py:311
  222.2 5.4 %collective-permute-start.37 = (f32[480,256]{1,0:T(8,128)S(1)}, f32[480,256]{1,0:T(8,128)S(1)}, u32[]{:S(2)}, u32[]{:S(2)}) collective-permute-start(f32[480,256]{1,0:T(8,128)S(1)} %constant_dynamic-slice_fusion.3), channel_id=1, source_target_pairs={{0,1},{1,0},{2,3},{3,2},{4,5},{5,4},{6,7},{7,6},{8,9},{9,8},{10,11... | collective-permute-start | bytes 1474568 | tf_op jit(solution)/shard_map/ppermute | solution.py:33
  227.6 1.5 collective-permute-done.37
  229.2 2.6 collective-permute-start.38
  231.8 1.5 collective-permute-start.39
  236.1 2.3 collective-permute-done.39
  239.2 12.2 %collective-permute-start.42 = (f32[192,256]{1,0:T(8,128)S(1)}, f32[192,256]{1,0:T(8,128)S(1)}, u32[]{:S(2)}, u32[]{:S(2)}) collective-permute-start(f32[192,256]{1,0:T(8,128)S(1)} %get-tuple-element.69), channel_id=1, source_target_pairs={{0,4},{1,5},{2,6},{3,7},{4,0},{5,1},{6,2},{7,3},{8,12},{9,13},{10,... | collective-permute-start | bytes 589832 | tf_op jit(solution)/shard_map/ppermute | solution.py:29
  251.4 1.7 collective-permute-start.43
  253.2 2.1 collective-permute-done.42
  255.3 4.3 %collective-permute-done.43 = f32[192,256]{1,0:T(8,128)S(1)} collective-permute-done((f32[192,256]{1,0:T(8,128)S(1)}, f32[192,256]{1,0:T(8,128)S(1)}, u32[]{:S(2)}, u32[]{:S(2)}) %collective-permute-start.43) | collective-permute-done | bytes 196640 | tf_op jit(solution)/shard_map/ppermute | solution.py:29
  259.6 2.0 collective-permute-start.44
  261.7 1.9 collective-permute-done.44
  264.6 3.5 %all-to-all-start = ((f32[16,16,256]{2,1,0:T(8,128)}), f32[16,16,256]{2,1,0:T(8,128)S(1)}, u32[]{:S(2)}, u32[]{:S(2)}) async-start(f32[16,16,256]{2,1,0:T(8,128)} %bitcast.4), calls=%async_computation | async-start | bytes 524288 | tf_op jit(solution)/shard_map/all_to_all | solution.py:524
  268.1 14.1 %factors.1 = (f32[256,256]{1,0:T(8,128)S(1)}, f32[256,256]{1,0:T(8,128)S(1)}, f32[8,128]{1,0:T(8,128)S(1)}) custom-call(f32[1536,256]{1,0:T(8,128)S(1)} %pad_maximum_fusion.right), custom_call_target="tpu_custom_call" | custom-call | tf_op jit(solution)/shard_map/factors/pallas_call | solution.py:431
  282.3 1.9 copy-done.5
  284.2 10.5 %last_update.1 = f32[384,3072]{1,0:T(8,128)} custom-call(f32[256,3072]{1,0:T(8,128)S(1)} %copy-done.5, f32[384,3072]{1,0:T(8,128)} %weight.5, f32[256,3968]{1,0:T(8,128)} %all-gather.5.cloned.1.call-done.whole.range_grad, f32[1536,256]{1,0:T(8,128)S(1)} %pad_maximum_fusion.right, f32[256,256]{1,0:T(8,128)S(1)} %bitcast.7, ...), custom_call_target="tpu_custom_call" | custom-call | tf_op jit(solution)/shard_map/last_update/pallas_call | solution.py:467
  (122 shorter events, 26.1 us)
Async XLA Ops:
  6.5 204.4 %all-gather.5.cloned.1.call-start = ((), (), s32[]{:S(2)}) async-start(), calls=%async_computation.2 | async-start | bytes 4317184 | tf_op jit(solution)/shard_map/all_gather | solution.py:504
  6.5 1.7 copy-start
  8.2 1.4 copy-start.3
  9.6 1.0 copy-start.8
  10.6 7.1 %copy-start.1 = (bf16[1536,768]{1,0:T(8,128)(2,1)S(1)}, bf16[1536,768]{1,0:T(8,128)(2,1)}, u32[]{:S(2)}) copy-start(bf16[1536,768]{1,0:T(8,128)(2,1)} %acts.5) | copy-start | bytes 7077892
  10.6 7.1 %copy-start.9 = (bf16[768,256]{1,0:T(8,128)(2,1)S(1)}, bf16[768,256]{1,0:T(8,128)(2,1)}, u32[]{:S(2)}) copy-start(bf16[768,256]{1,0:T(8,128)(2,1)} %sketch_in.3) | copy-start | bytes 1179652
  16.3 8.7 %collective-permute-start = (f32[768,512]{1,0:T(8,128)}, f32[768,512]{1,0:T(8,128)}, u32[]{:S(2)}, u32[]{:S(2)}) collective-permute-start(f32[768,512]{1,0:T(8,128)} %get-tuple-element.17), channel_id=1, source_target_pairs={{0,1},{1,0},{2,3},{3,2},{4,5},{5,4},{6,7},{7,6},{8,9},{9,8},{10,11... | collective-permute-start | bytes 4718600 | tf_op jit(solution)/shard_map/ppermute | solution.py:33
  17.8 1.4 copy-start.4
  23.9 1.1 copy-start.10
  27.3 12.4 %collective-permute-start.1 = (f32[192,512]{1,0:T(8,128)S(1)}, f32[192,512]{1,0:T(8,128)S(1)}, u32[]{:S(2)}, u32[]{:S(2)}) collective-permute-start(f32[192,512]{1,0:T(8,128)S(1)} %get-tuple-element.46), channel_id=1, source_target_pairs={{0,4},{1,5},{2,6},{3,7},{4,0},{5,1},{6,2},{7,3},{8,12},{9,13},{10,... | collective-permute-start | bytes 1179656 | tf_op jit(solution)/shard_map/ppermute | solution.py:29
  30.2 18.2 %collective-permute-start.3 = (f32[192,512]{1,0:T(8,128)S(1)}, f32[192,512]{1,0:T(8,128)S(1)}, u32[]{:S(2)}, u32[]{:S(2)}) collective-permute-start(f32[192,512]{1,0:T(8,128)S(1)} %get-tuple-element.47), channel_id=1, source_target_pairs={{0,6},{1,7},{2,0},{3,1},{4,2},{5,3},{6,4},{7,5},{8,14},{9,15},{10,... | collective-permute-start | bytes 1179656 | tf_op jit(solution)/shard_map/ppermute | solution.py:29
  31.1 17.4 %collective-permute-start.2 = (f32[192,512]{1,0:T(8,128)S(1)}, f32[192,512]{1,0:T(8,128)}, u32[]{:S(2)}, u32[]{:S(2)}) collective-permute-start(f32[192,512]{1,0:T(8,128)S(1)} %get-tuple-element.48), channel_id=1, source_target_pairs={{0,2},{1,3},{2,4},{3,5},{4,6},{5,7},{6,0},{7,1},{8,10},{9,11},{10,... | collective-permute-start | bytes 1179656 | tf_op jit(solution)/shard_map/ppermute | solution.py:29
  39.7 8.7 %copy-start.12 = (f32[192,512]{1,0:T(8,128)}, f32[192,512]{1,0:T(8,128)S(1)}, u32[]{:S(2)}) copy-start(f32[192,512]{1,0:T(8,128)S(1)} %collective-permute-done.1) | copy-start | bytes 1179652
  48.4 0.7 copy-start.14
  49.2 1.0 copy-start.13
  51.4 11.3 %collective-permute-start.4 = (f32[192,512]{1,0:T(8,128)S(1)}, f32[192,512]{1,0:T(8,128)S(1)}, u32[]{:S(2)}, u32[]{:S(2)}) collective-permute-start(f32[192,512]{1,0:T(8,128)S(1)} %get-tuple-element.28), channel_id=1, source_target_pairs={{0,2},{1,3},{2,4},{3,5},{4,6},{5,7},{6,0},{7,1},{8,10},{9,11},{10,... | collective-permute-start | bytes 1179656 | tf_op jit(solution)/shard_map/ppermute | solution.py:29
  52.9 19.5 %collective-permute-start.5 = (f32[192,512]{1,0:T(8,128)S(1)}, f32[192,512]{1,0:T(8,128)S(1)}, u32[]{:S(2)}, u32[]{:S(2)}) collective-permute-start(f32[192,512]{1,0:T(8,128)S(1)} %get-tuple-element.28), channel_id=1, source_target_pairs={{0,4},{1,5},{2,6},{3,7},{4,0},{5,1},{6,2},{7,3},{8,12},{9,13},{10,... | collective-permute-start | bytes 1179656 | tf_op jit(solution)/shard_map/ppermute | solution.py:29
  55.2 17.2 %collective-permute-start.6 = (f32[192,512]{1,0:T(8,128)S(1)}, f32[192,512]{1,0:T(8,128)S(1)}, u32[]{:S(2)}, u32[]{:S(2)}) collective-permute-start(f32[192,512]{1,0:T(8,128)S(1)} %get-tuple-element.28), channel_id=1, source_target_pairs={{0,6},{1,7},{2,0},{3,1},{4,2},{5,3},{6,4},{7,5},{8,14},{9,15},{10,... | collective-permute-start | bytes 1179656 | tf_op jit(solution)/shard_map/ppermute | solution.py:29
  72.5 4.4 %collective-permute-start.7 = (f32[768,512]{1,0:T(8,128)S(1)}, f32[768,512]{1,0:T(8,128)S(1)}, u32[]{:S(2)}, u32[]{:S(2)}) collective-permute-start(f32[768,512]{1,0:T(8,128)S(1)} %constant_dynamic-update-slice_fusion.8.own), channel_id=1, source_target_pairs={{0,1},{1,0},{2,3},{3,2},{4,5},{5,4},{6,7},{7,6},{8,9},{9,8},{10,11... | collective-permute-start | bytes 4718600 | tf_op jit(solution)/shard_map/ppermute | solution.py:33
  89.5 1.3 copy-start.6
  90.8 5.6 %copy-start.11 = (f32[128,3968]{1,0:T(8,128)S(1)}, f32[128,3968]{1,0:T(8,128)}, u32[]{:S(2)}) copy-start(f32[128,3968]{1,0:T(8,128)} %get-tuple-element.21) | copy-start | bytes 6094852
  92.0 14.5 %collective-permute-start.8 = (f32[32,3968]{1,0:T(8,128)}, f32[32,3968]{1,0:T(8,128)S(1)}, u32[]{:S(2)}, u32[]{:S(2)}) collective-permute-start(f32[32,3968]{1,0:T(8,128)} %get-tuple-element.35), channel_id=1, source_target_pairs={{0,16},{8,24},{16,0},{24,8},{32,48},{40,56},{48,32},{56,40},{64,80... | collective-permute-start | bytes 1523720 | tf_op jit(solution)/shard_map/ppermute | solution.py:29
  94.9 22.9 %collective-permute-start.10 = (f32[32,3968]{1,0:T(8,128)}, f32[32,3968]{1,0:T(8,128)S(1)}, u32[]{:S(2)}, u32[]{:S(2)}) collective-permute-start(f32[32,3968]{1,0:T(8,128)} %get-tuple-element.36), channel_id=1, source_target_pairs={{0,24},{8,0},{16,8},{24,16},{32,56},{40,32},{48,40},{56,48},{64,88... | collective-permute-start | bytes 1523720 | tf_op jit(solution)/shard_map/ppermute | solution.py:29
  95.6 22.4 %collective-permute-start.9 = (f32[32,3968]{1,0:T(8,128)}, f32[32,3968]{1,0:T(8,128)S(1)}, u32[]{:S(2)}, u32[]{:S(2)}) collective-permute-start(f32[32,3968]{1,0:T(8,128)} %get-tuple-element.37), channel_id=1, source_target_pairs={{0,8},{8,16},{16,24},{24,0},{32,40},{40,48},{48,56},{56,32},{64,72... | collective-permute-start | bytes 1523720 | tf_op jit(solution)/shard_map/ppermute | solution.py:29
  96.4 27.1 %collective-permute-start.14 = (f32[32,3968]{1,0:T(8,128)S(1)}, f32[32,3968]{1,0:T(8,128)S(1)}, u32[]{:S(2)}, u32[]{:S(2)}) collective-permute-start(f32[32,3968]{1,0:T(8,128)S(1)} %get-tuple-element.32), channel_id=1, source_target_pairs={{0,64},{8,72},{16,80},{24,88},{32,96},{40,104},{48,112},{56,120},{... | collective-permute-start | bytes 1523720 | tf_op jit(solution)/shard_map/ppermute | solution.py:29
  100.1 24.5 %collective-permute-start.16 = (f32[32,3968]{1,0:T(8,128)S(1)}, f32[32,3968]{1,0:T(8,128)S(1)}, u32[]{:S(2)}, u32[]{:S(2)}) collective-permute-start(f32[32,3968]{1,0:T(8,128)S(1)} %get-tuple-element.33), channel_id=1, source_target_pairs={{0,96},{8,104},{16,112},{24,120},{32,0},{40,8},{48,16},{56,24},{64... | collective-permute-start | bytes 1523720 | tf_op jit(solution)/shard_map/ppermute | solution.py:29
  106.5 18.1 %collective-permute-start.15 = (f32[32,3968]{1,0:T(8,128)S(1)}, f32[32,3968]{1,0:T(8,128)S(1)}, u32[]{:S(2)}, u32[]{:S(2)}) collective-permute-start(f32[32,3968]{1,0:T(8,128)S(1)} %get-tuple-element.34), channel_id=1, source_target_pairs={{0,32},{8,40},{16,48},{24,56},{32,64},{40,72},{48,80},{56,88},{64,... | collective-permute-start | bytes 1523720 | tf_op jit(solution)/shard_map/ppermute | solution.py:29
  119.2 9.3 %collective-permute-start.11 = (f32[8,3968]{1,0:T(8,128)S(1)}, f32[8,3968]{1,0:T(8,128)S(1)}, u32[]{:S(2)}, u32[]{:S(2)}) collective-permute-start(f32[8,3968]{1,0:T(8,128)S(1)} %get-tuple-element.52), channel_id=1, source_target_pairs={{0,64},{8,72},{16,80},{24,88},{32,96},{40,104},{48,112},{56,120},{... | collective-permute-start | bytes 380936 | tf_op jit(solution)/shard_map/ppermute | solution.py:29
  122.9 6.3 %collective-permute-start.13 = (f32[8,3968]{1,0:T(8,128)S(1)}, f32[8,3968]{1,0:T(8,128)S(1)}, u32[]{:S(2)}, u32[]{:S(2)}) collective-permute-start(f32[8,3968]{1,0:T(8,128)S(1)} %get-tuple-element.53), channel_id=1, source_target_pairs={{0,96},{8,104},{16,112},{24,120},{32,0},{40,8},{48,16},{56,24},{64... | collective-permute-start | bytes 380936 | tf_op jit(solution)/shard_map/ppermute | solution.py:29
  123.6 5.7 %collective-permute-start.12 = (f32[8,3968]{1,0:T(8,128)S(1)}, f32[8,3968]{1,0:T(8,128)S(1)}, u32[]{:S(2)}, u32[]{:S(2)}) collective-permute-start(f32[8,3968]{1,0:T(8,128)S(1)} %get-tuple-element.54), channel_id=1, source_target_pairs={{0,32},{8,40},{16,48},{24,56},{32,64},{40,72},{48,80},{56,88},{64,... | collective-permute-start | bytes 380936 | tf_op jit(solution)/shard_map/ppermute | solution.py:29
  124.8 5.4 %collective-permute-start.17 = (f32[8,3968]{1,0:T(8,128)S(1)}, f32[8,3968]{1,0:T(8,128)S(1)}, u32[]{:S(2)}, u32[]{:S(2)}) collective-permute-start(f32[8,3968]{1,0:T(8,128)S(1)} %get-tuple-element.49), channel_id=1, source_target_pairs={{0,16},{8,24},{16,0},{24,8},{32,48},{40,56},{48,32},{56,40},{64,80... | collective-permute-start | bytes 380936 | tf_op jit(solution)/shard_map/ppermute | solution.py:29
  127.7 5.2 %collective-permute-start.19 = (f32[8,3968]{1,0:T(8,128)S(1)}, f32[8,3968]{1,0:T(8,128)S(1)}, u32[]{:S(2)}, u32[]{:S(2)}) collective-permute-start(f32[8,3968]{1,0:T(8,128)S(1)} %get-tuple-element.50), channel_id=1, source_target_pairs={{0,24},{8,0},{16,8},{24,16},{32,56},{40,32},{48,40},{56,48},{64,88... | collective-permute-start | bytes 380936 | tf_op jit(solution)/shard_map/ppermute | solution.py:29
  128.5 5.6 %collective-permute-start.18 = (f32[8,3968]{1,0:T(8,128)S(1)}, f32[8,3968]{1,0:T(8,128)S(1)}, u32[]{:S(2)}, u32[]{:S(2)}) collective-permute-start(f32[8,3968]{1,0:T(8,128)S(1)} %get-tuple-element.51), channel_id=1, source_target_pairs={{0,8},{8,16},{16,24},{24,0},{32,40},{40,48},{48,56},{56,32},{64,72... | collective-permute-start | bytes 380936 | tf_op jit(solution)/shard_map/ppermute | solution.py:29
  134.9 147.3 %all-gather.3.cloned.1.call-start = ((), (), s32[]{:S(2)}) async-start(), calls=%async_computation.1 | async-start | bytes 3342336 | tf_op jit(solution)/shard_map/all_gather | solution.py:516
  135.0 6.8 %collective-permute-start.20 = (f32[48,256]{1,0:T(8,128)S(1)}, f32[48,256]{1,0:T(8,128)S(1)}, u32[]{:S(2)}, u32[]{:S(2)}) collective-permute-start(f32[48,256]{1,0:T(8,128)S(1)} %pad_maximum_fusion.4), channel_id=1, source_target_pairs={{0,0},{1,16},{2,32},{3,48},{4,64},{5,80},{6,96},{7,112},{8,2},{9,1... | collective-permute-start | bytes 147464 | tf_op jit(solution)/shard_map/ppermute | solution.py:513
  141.9 10.3 %collective-permute-start.23 = (f32[48,256]{1,0:T(8,128)S(1)}, f32[48,256]{1,0:T(8,128)S(1)}, u32[]{:S(2)}, u32[]{:S(2)}) collective-permute-start(f32[48,256]{1,0:T(8,128)S(1)} %collective-permute-done.20), channel_id=1, source_target_pairs={{0,6},{1,7},{2,0},{3,1},{4,2},{5,3},{6,4},{7,5},{8,14},{9,15},{10,... | collective-permute-start | bytes 147464 | tf_op jit(solution)/shard_map/ppermute | solution.py:29
  147.1 5.1 %collective-permute-start.22 = (f32[48,256]{1,0:T(8,128)S(1)}, f32[48,256]{1,0:T(8,128)S(1)}, u32[]{:S(2)}, u32[]{:S(2)}) collective-permute-start(f32[48,256]{1,0:T(8,128)S(1)} %collective-permute-done.20), channel_id=1, source_target_pairs={{0,4},{1,5},{2,6},{3,7},{4,0},{5,1},{6,2},{7,3},{8,12},{9,13},{10,... | collective-permute-start | bytes 147464 | tf_op jit(solution)/shard_map/ppermute | solution.py:29
  147.1 5.1 %collective-permute-start.21 = (f32[48,256]{1,0:T(8,128)S(1)}, f32[48,256]{1,0:T(8,128)S(1)}, u32[]{:S(2)}, u32[]{:S(2)}) collective-permute-start(f32[48,256]{1,0:T(8,128)S(1)} %collective-permute-done.20), channel_id=1, source_target_pairs={{0,2},{1,3},{2,4},{3,5},{4,6},{5,7},{6,0},{7,1},{8,10},{9,11},{10,... | collective-permute-start | bytes 147464 | tf_op jit(solution)/shard_map/ppermute | solution.py:29
  152.2 4.1 %collective-permute-start.24 = (f32[192,256]{1,0:T(8,128)S(1)}, f32[192,256]{1,0:T(8,128)S(1)}, u32[]{:S(2)}, u32[]{:S(2)}) collective-permute-start(f32[192,256]{1,0:T(8,128)S(1)} %constant_dynamic-update-slice_fusion.4), channel_id=1, source_target_pairs={{0,1},{1,0},{2,3},{3,2},{4,5},{5,4},{6,7},{7,6},{8,9},{9,8},{10,11... | collective-permute-start | bytes 589832 | tf_op jit(solution)/shard_map/ppermute | solution.py:33
  162.3 16.8 %collective-permute-start.25 = (f32[32,3072]{1,0:T(8,128)S(1)}, f32[32,3072]{1,0:T(8,128)S(1)}, u32[]{:S(2)}, u32[]{:S(2)}) collective-permute-start(f32[32,3072]{1,0:T(8,128)S(1)} %get-tuple-element.40), channel_id=1, source_target_pairs={{0,16},{8,24},{16,0},{24,8},{32,48},{40,56},{48,32},{56,40},{64,80... | collective-permute-start | bytes 1179656 | tf_op jit(solution)/shard_map/ppermute | solution.py:29
  162.4 31.5 %collective-permute-start.27 = (f32[32,3072]{1,0:T(8,128)S(1)}, f32[32,3072]{1,0:T(8,128)S(1)}, u32[]{:S(2)}, u32[]{:S(2)}) collective-permute-start(f32[32,3072]{1,0:T(8,128)S(1)} %get-tuple-element.41), channel_id=1, source_target_pairs={{0,24},{8,0},{16,8},{24,16},{32,56},{40,32},{48,40},{56,48},{64,88... | collective-permute-start | bytes 1179656 | tf_op jit(solution)/shard_map/ppermute | solution.py:29
  167.3 26.7 %collective-permute-start.26 = (f32[32,3072]{1,0:T(8,128)S(1)}, f32[32,3072]{1,0:T(8,128)S(1)}, u32[]{:S(2)}, u32[]{:S(2)}) collective-permute-start(f32[32,3072]{1,0:T(8,128)S(1)} %get-tuple-element.42), channel_id=1, source_target_pairs={{0,8},{8,16},{16,24},{24,0},{32,40},{40,48},{48,56},{56,32},{64,72... | collective-permute-start | bytes 1179656 | tf_op jit(solution)/shard_map/ppermute | solution.py:29
  167.4 30.9 %collective-permute-start.31 = (f32[32,3072]{1,0:T(8,128)S(1)}, f32[32,3072]{1,0:T(8,128)S(1)}, u32[]{:S(2)}, u32[]{:S(2)}) collective-permute-start(f32[32,3072]{1,0:T(8,128)S(1)} %get-tuple-element.43), channel_id=1, source_target_pairs={{0,64},{8,72},{16,80},{24,88},{32,96},{40,104},{48,112},{56,120},{... | collective-permute-start | bytes 1179656 | tf_op jit(solution)/shard_map/ppermute | solution.py:29
  167.5 32.4 %collective-permute-start.33 = (f32[32,3072]{1,0:T(8,128)S(1)}, f32[32,3072]{1,0:T(8,128)S(1)}, u32[]{:S(2)}, u32[]{:S(2)}) collective-permute-start(f32[32,3072]{1,0:T(8,128)S(1)} %get-tuple-element.44), channel_id=1, source_target_pairs={{0,96},{8,104},{16,112},{24,120},{32,0},{40,8},{48,16},{56,24},{64... | collective-permute-start | bytes 1179656 | tf_op jit(solution)/shard_map/ppermute | solution.py:29
  179.1 22.4 %collective-permute-start.32 = (f32[32,3072]{1,0:T(8,128)S(1)}, f32[32,3072]{1,0:T(8,128)S(1)}, u32[]{:S(2)}, u32[]{:S(2)}) collective-permute-start(f32[32,3072]{1,0:T(8,128)S(1)} %get-tuple-element.45), channel_id=1, source_target_pairs={{0,32},{8,40},{16,48},{24,56},{32,64},{40,72},{48,80},{56,88},{64,... | collective-permute-start | bytes 1179656 | tf_op jit(solution)/shard_map/ppermute | solution.py:29
  194.1 11.4 %collective-permute-start.28 = (f32[8,3072]{1,0:T(8,128)S(1)}, f32[8,3072]{1,0:T(8,128)S(1)}, u32[]{:S(2)}, u32[]{:S(2)}) collective-permute-start(f32[8,3072]{1,0:T(8,128)S(1)} %get-tuple-element.58), channel_id=1, source_target_pairs={{0,64},{8,72},{16,80},{24,88},{32,96},{40,104},{48,112},{56,120},{... | collective-permute-start | bytes 294920 | tf_op jit(solution)/shard_map/ppermute | solution.py:29
  195.0 11.1 %collective-permute-start.30 = (f32[8,3072]{1,0:T(8,128)S(1)}, f32[8,3072]{1,0:T(8,128)S(1)}, u32[]{:S(2)}, u32[]{:S(2)}) collective-permute-start(f32[8,3072]{1,0:T(8,128)S(1)} %get-tuple-element.59), channel_id=1, source_target_pairs={{0,96},{8,104},{16,112},{24,120},{32,0},{40,8},{48,16},{56,24},{64... | collective-permute-start | bytes 294920 | tf_op jit(solution)/shard_map/ppermute | solution.py:29
  198.3 7.8 %collective-permute-start.29 = (f32[8,3072]{1,0:T(8,128)S(1)}, f32[8,3072]{1,0:T(8,128)S(1)}, u32[]{:S(2)}, u32[]{:S(2)}) collective-permute-start(f32[8,3072]{1,0:T(8,128)S(1)} %get-tuple-element.60), channel_id=1, source_target_pairs={{0,32},{8,40},{16,48},{24,56},{32,64},{40,72},{48,80},{56,88},{64,... | collective-permute-start | bytes 294920 | tf_op jit(solution)/shard_map/ppermute | solution.py:29
  201.6 5.1 %collective-permute-start.34 = (f32[8,3072]{1,0:T(8,128)S(1)}, f32[8,3072]{1,0:T(8,128)S(1)}, u32[]{:S(2)}, u32[]{:S(2)}) collective-permute-start(f32[8,3072]{1,0:T(8,128)S(1)} %get-tuple-element.61), channel_id=1, source_target_pairs={{0,16},{8,24},{16,0},{24,8},{32,48},{40,56},{48,32},{56,40},{64,80... | collective-permute-start | bytes 294920 | tf_op jit(solution)/shard_map/ppermute | solution.py:29
  204.5 4.1 %collective-permute-start.36 = (f32[8,3072]{1,0:T(8,128)S(1)}, f32[8,3072]{1,0:T(8,128)S(1)}, u32[]{:S(2)}, u32[]{:S(2)}) collective-permute-start(f32[8,3072]{1,0:T(8,128)S(1)} %get-tuple-element.62), channel_id=1, source_target_pairs={{0,24},{8,0},{16,8},{24,16},{32,56},{40,32},{48,40},{56,48},{64,88... | collective-permute-start | bytes 294920 | tf_op jit(solution)/shard_map/ppermute | solution.py:29
  205.5 4.7 %collective-permute-start.35 = (f32[8,3072]{1,0:T(8,128)S(1)}, f32[8,3072]{1,0:T(8,128)S(1)}, u32[]{:S(2)}, u32[]{:S(2)}) collective-permute-start(f32[8,3072]{1,0:T(8,128)S(1)} %get-tuple-element.63), channel_id=1, source_target_pairs={{0,8},{8,16},{16,24},{24,0},{32,40},{40,48},{48,56},{56,32},{64,72... | collective-permute-start | bytes 294920 | tf_op jit(solution)/shard_map/ppermute | solution.py:29
  210.9 1.3 copy-start.7
  212.2 2.2 copy-start.2
  222.2 6.9 %collective-permute-start.37 = (f32[480,256]{1,0:T(8,128)S(1)}, f32[480,256]{1,0:T(8,128)S(1)}, u32[]{:S(2)}, u32[]{:S(2)}) collective-permute-start(f32[480,256]{1,0:T(8,128)S(1)} %constant_dynamic-slice_fusion.3), channel_id=1, source_target_pairs={{0,1},{1,0},{2,3},{3,2},{4,5},{5,4},{6,7},{7,6},{8,9},{9,8},{10,11... | collective-permute-start | bytes 1474568 | tf_op jit(solution)/shard_map/ppermute | solution.py:33
  229.2 6.1 %collective-permute-start.38 = (f32[120,256]{1,0:T(8,128)S(1)}, f32[120,256]{1,0:T(8,128)S(1)}, u32[]{:S(2)}, u32[]{:S(2)}) collective-permute-start(f32[120,256]{1,0:T(8,128)S(1)} %get-tuple-element.55), channel_id=1, source_target_pairs={{0,4},{1,5},{2,6},{3,7},{4,0},{5,1},{6,2},{7,3},{8,12},{9,13},{10,... | collective-permute-start | bytes 368648 | tf_op jit(solution)/shard_map/ppermute | solution.py:29
  231.8 4.3 %collective-permute-start.40 = (f32[120,256]{1,0:T(8,128)S(1)}, f32[120,256]{1,0:T(8,128)S(1)}, u32[]{:S(2)}, u32[]{:S(2)}) collective-permute-start(f32[120,256]{1,0:T(8,128)S(1)} %get-tuple-element.56), channel_id=1, source_target_pairs={{0,6},{1,7},{2,0},{3,1},{4,2},{5,3},{6,4},{7,5},{8,14},{9,15},{10,... | collective-permute-start | bytes 368648 | tf_op jit(solution)/shard_map/ppermute | solution.py:29
  231.8 6.6 %collective-permute-start.39 = (f32[120,256]{1,0:T(8,128)S(1)}, f32[120,256]{1,0:T(8,128)S(1)}, u32[]{:S(2)}, u32[]{:S(2)}) collective-permute-start(f32[120,256]{1,0:T(8,128)S(1)} %get-tuple-element.57), channel_id=1, source_target_pairs={{0,2},{1,3},{2,4},{3,5},{4,6},{5,7},{6,0},{7,1},{8,10},{9,11},{10,... | collective-permute-start | bytes 368648 | tf_op jit(solution)/shard_map/ppermute | solution.py:29
  238.6 14.6 %collective-permute-start.41 = (f32[192,256]{1,0:T(8,128)S(1)}, f32[192,256]{1,0:T(8,128)S(1)}, u32[]{:S(2)}, u32[]{:S(2)}) collective-permute-start(f32[192,256]{1,0:T(8,128)S(1)} %get-tuple-element.69), channel_id=1, source_target_pairs={{0,2},{1,3},{2,4},{3,5},{4,6},{5,7},{6,0},{7,1},{8,10},{9,11},{10,... | collective-permute-start | bytes 589832 | tf_op jit(solution)/shard_map/ppermute | solution.py:29
  239.2 16.0 %collective-permute-start.42 = (f32[192,256]{1,0:T(8,128)S(1)}, f32[192,256]{1,0:T(8,128)S(1)}, u32[]{:S(2)}, u32[]{:S(2)}) collective-permute-start(f32[192,256]{1,0:T(8,128)S(1)} %get-tuple-element.69), channel_id=1, source_target_pairs={{0,4},{1,5},{2,6},{3,7},{4,0},{5,1},{6,2},{7,3},{8,12},{9,13},{10,... | collective-permute-start | bytes 589832 | tf_op jit(solution)/shard_map/ppermute | solution.py:29
  251.4 8.2 %collective-permute-start.43 = (f32[192,256]{1,0:T(8,128)S(1)}, f32[192,256]{1,0:T(8,128)S(1)}, u32[]{:S(2)}, u32[]{:S(2)}) collective-permute-start(f32[192,256]{1,0:T(8,128)S(1)} %get-tuple-element.69), channel_id=1, source_target_pairs={{0,6},{1,7},{2,0},{3,1},{4,2},{5,3},{6,4},{7,5},{8,14},{9,15},{10,... | collective-permute-start | bytes 589832 | tf_op jit(solution)/shard_map/ppermute | solution.py:29
  259.6 4.0 %collective-permute-start.44 = (f32[768,256]{1,0:T(8,128)S(1)}, f32[768,256]{1,0:T(8,128)S(1)}, u32[]{:S(2)}, u32[]{:S(2)}) collective-permute-start(f32[768,256]{1,0:T(8,128)S(1)} %constant_dynamic-update-slice_fusion), channel_id=1, source_target_pairs={{0,1},{1,0},{2,3},{3,2},{4,5},{5,4},{6,7},{7,6},{8,9},{9,8},{10,11... | collective-permute-start | bytes 2359304 | tf_op jit(solution)/shard_map/ppermute | solution.py:33
  264.6 17.7 %all-to-all-start = ((f32[16,16,256]{2,1,0:T(8,128)}), f32[16,16,256]{2,1,0:T(8,128)S(1)}, u32[]{:S(2)}, u32[]{:S(2)}) async-start(f32[16,16,256]{2,1,0:T(8,128)} %bitcast.4), calls=%async_computation | async-start | bytes 524288 | tf_op jit(solution)/shard_map/all_to_all | solution.py:524
  282.3 1.9 copy-start.5
Sparse Core Ops, SparseCore 0:
  135.1 67.3 all-gather.4
  211.0 48.5 all-gather.2

commit v2 on v1

--- a/solution.py
+++ b/solution.py
@@ -64,7 +64,8 @@
 
 def scatter_dp(first, second):
     first, second = scatter_four(first, "y"), scatter_four(second, "z")
-    return jnp.concatenate([scatter_four(first, "z"), scatter_four(second, "y")])
+    both = [scatter_four(first, "z"), scatter_four(second, "y")]
+    return jnp.concatenate(both), second
 
 
 def store_groups(first, second, columns, value):
@@ -83,6 +84,11 @@
     core, half = lax.axis_index("tensor") % 2, value.shape[0] // 2
     other = swap_cores(rows(value, 1 - core, half))
     return scatter_four(rows(value, core, half) + other, "x")
+
+
+def exchange_x(value):
+    groups = [[2 * x + core for x in range(4)] for core in range(2)]
+    return lax.all_to_all(value, "tensor", 0, 0, axis_index_groups=groups, tiled=True)
 
 
 def gather_tensor(value):
@@ -110,11 +116,11 @@
     )
 
 
-def call(kernel, out_shape, **options):
+def call(kernel, out_shape, vmem=VMEM_LIMIT, **options):
     return pl.pallas_call(
         kernel,
         out_shape=out_shape,
-        compiler_params=pltpu.CompilerParams(vmem_limit_bytes=VMEM_LIMIT),
+        compiler_params=pltpu.CompilerParams(vmem_limit_bytes=vmem),
         **options,
     )
 
@@ -172,6 +178,7 @@
     return call(
         sketch_kernel,
         [array(count, 2 * R), array(16, 128)],
+        vmem=60 * 1024 * 1024,
         grid_spec=grid_spec,
         name="sketches",
     )(half.astype(jnp.int32).reshape(1), grads, acts, sketch_out, sketch_in)
@@ -286,48 +293,74 @@
     )(rows_act, weight)
 
 
-def right_kernel(whole, one, two, three, weight, left, sums):
+def right_kernel(whole, *refs):
+    extra, (weight, after, sums) = refs[:6], refs[6:]
+
     @pl.when(pl.program_id(0) == 0)
     def _():
         sums[...] = jnp.zeros_like(sums)
-        pieces = split(jnp.concatenate([one[...], two[...], three[...]]))
+        blocks = [jnp.concatenate([extra[i][...], extra[i + 1][...]], axis=1) for i in (0, 2, 4)]
+        pieces = split(jnp.concatenate(blocks))
         gram = product(pieces, pieces, ((0,), (0,)))
         for i in range(8):
-            sums[i * 120 + 80 : i * 120 + 112, :] = gram[i * 32 : i * 32 + 32]
+            sums[i * 112 + 80 : i * 112 + 112, :] = gram[i * 32 : i * 32 + 32]
 
     ranges = split(whole[...])
     right = product(split(weight[...]), ranges, LAST)
     gram = product(ranges, ranges, LAST)
-    both = product(split(left[...]), ranges, LAST)
     for i in range(8):
-        at = i * 120
+        at = i * 112
         sums[at : at + 48, :] += right[i * 48 : i * 48 + 48]
         sums[at + 48 : at + 80, :] += gram[i * 32 : i * 32 + 32]
-        sums[at + 112 : at + 114, :] += both[i * 2 : i * 2 + 2]
-
-
-def right_products(whole, extra, weight, left):
+
+
+def right_products(gathered, weight, after):
     count, columns = weight.shape
+    extra = lambda i: pl.BlockSpec((R, 128), lambda j: (0, columns // 128 + 1 + i))
     return call(
         right_kernel,
-        array(960, R),
+        array(896, R),
         grid=(columns // TILE,),
         in_specs=[pl.BlockSpec((R, TILE), lambda j: (0, j))]
-        + [pl.BlockSpec((R, R), lambda j: (0, 0))] * 3
+        + [extra(i) for i in range(6)]
         + [
             pl.BlockSpec((count, TILE), lambda j: (0, j)),
-            pl.BlockSpec((16, TILE), lambda j: (0, j)),
-        ],
-        out_specs=pl.BlockSpec((960, R), lambda j: (0, 0)),
+            pl.BlockSpec(memory_space=pl.ANY),
+        ],
+        out_specs=pl.BlockSpec((896, R), lambda j: (0, 0)),
         name="right_products",
-    )(whole, *extra, weight, left)
+    )(*[gathered] * 7, weight, after)
+
+
+def both_kernel(whole, left, out):
+    @pl.when(pl.program_id(0) == 0)
+    def _():
+        out[...] = jnp.zeros_like(out)
+
+    out[...] += product(split(left[...]), split(whole[...]), LAST)
+
+
+def both_products(gathered, left):
+    count, columns = left.shape
+    return call(
+        both_kernel,
+        array(count, R),
+        grid=(columns // 1024,),
+        in_specs=[
+            pl.BlockSpec((R, 1024), lambda j: (0, j)),
+            pl.BlockSpec((count, 1024), lambda j: (0, j)),
+        ],
+        out_specs=pl.BlockSpec((count, R), lambda j: (0, 0)),
+        name="both_products",
+    )(gathered, left)
 
 
 def pack_kernel(right, out):
+    total = right[184:200, :]
+    for i in range(1, 8):
+        total += right[i * 200 + 184 : i * 200 + 200, :]
     for d in range(16):
-        for i in range(8):
-            at = 16 * d + 2 * i
-            out[at : at + 2, :] = right[i * 192 + 112 : i * 192 + 114, :]
+        out[16 * d : 16 * d + 16, :] = total
 
 
 def pack(right):
@@ -408,7 +441,7 @@
 def factor_kernel(counts, right, inverse_act, inverse_grad, scale, *work):
     trace_grad, trace_act = jnp.zeros((1, 1)), jnp.zeros((1, 1))
     for i in range(8):
-        at = i * 192 + 184
+        at = i * 200 + 176
         trace_grad += right[at : at + 1, 64:65]
         trace_act += right[at : at + 1, 65:66]
     damp_grad = DAMPING * trace_grad / counts[0]
@@ -420,9 +453,9 @@
     for w in work:
         w[:, R:] = identity
     for i in range(8):
-        at, here = slice(i * 32, i * 32 + 32), i * 192
-        work[0][at, :R] = damp_act * right[here + 152 : here + 184, :] + right[here + 80 : here + 112, :]
-        work[1][at, :R] = damp_grad * right[here + 120 : here + 152, :] + right[here + 48 : here + 80, :]
+        at, here = slice(i * 32, i * 32 + 32), i * 200
+        work[0][at, :R] = damp_act * right[here + 144 : here + 176, :] + right[here + 80 : here + 112, :]
+        work[1][at, :R] = damp_grad * right[here + 112 : here + 144, :] + right[here + 48 : here + 80, :]
     lower_inverses(work, (inverse_act, inverse_grad))
 
 
@@ -450,7 +483,7 @@
     @pl.when(pl.program_id(0) == 0)
     def _():
         for i in range(8):
-            sums[i * 48 : i * 48 + 48, :] = right[i * 192 : i * 192 + 48, :]
+            sums[i * 48 : i * 48 + 48, :] = right[i * 200 : i * 200 + 48, :]
         solved = applied(rows_act[...], inverse_act[...])
         pieces[0][...], pieces[1][...] = split(solved)
         rest = sums[...] - product(split(solved), split(both[...]), INNER)
@@ -495,10 +528,12 @@
     part, sq_one = sketches(1 - core_id, grads_out, acts, sketch_out, sketch_in)
     other = swap_cores(part)
     part, sq_two = sketches(core_id, grads_out, acts, sketch_out, sketch_in)
-    own = gather_four(scatter_four(part + other, "x"), "x")
+    part = exchange_x(part + other)
+    part = jnp.sum(part.reshape(4, -1, 2 * R), axis=0)
+    own = exchange_x(jnp.tile(part, (4, 1)))
     other = swap_cores(own)
 
-    piece = scatter_dp(
+    piece, _ = scatter_dp(
         *ranges(places, own, other, grads_out, acts, sq_one, sq_two, tokens_all)
     )
     gathered = lax.all_gather(piece, "dp", axis=0, tiled=True)
@@ -512,15 +547,15 @@
             moves.append((d * 8 + t, (2 * t + d // 8) * 8 + 2 * (k % 4) + k // 4))
     rows_act = gather_tensor(lax.ppermute(piece, ("dp", "tensor"), moves))
 
-    piece = scatter_dp(*left_products(rows_act, weight_grad))
+    piece, after = scatter_dp(*left_products(rows_act, weight_grad))
     left_sums = lax.all_gather(piece, "dp", axis=0, tiled=True)
 
-    blocks = [gathered[:, at + i * R : at + i * R + R] for i in range(3)]
-    part = scatter_tensor(right_products(gathered, blocks, weight_grad, piece))
+    part = scatter_tensor(right_products(gathered, weight_grad, after))
     extra = gathered[:, columns:at]
     cores = extra[:, : 2 * width].T
     rest = jnp.pad(extra[:8], ((0, 0), (0, R - 128)))
-    right = gather_tensor(jnp.concatenate([part, cores, rest]))
+    part = jnp.concatenate([part, cores, rest, both_products(gathered, piece)])
+    right = gather_tensor(part)
     both = lax.all_to_all(pack(right), "dp", 0, 0, tiled=True)
 
     counts = (float(tokens_all * FF), float(tokens_all * D))

time: 307 us -> 302 us (0.984)
  blocking collectives: 0 us -> 46.6 us
  waiting for transfers between devices: 107 us -> 71.2 us
  starting transfers between devices: 93.6 us -> 83 us
  local copies, waits for them, and re-layouts: 18.5 us -> 11.2 us
  Pallas kernels: 62 us -> 65.5 us
    all_to_all x0 -> x2, blocking collectives: none -> 46.6 us  [exchange_x(): lax.all_to_all(value, 'tensor', 0, 0, axis_index_groups=groups, tiled=True)]
    ppermute x39 -> x33, waiting for transfers between devices: 97.8 us -> 62.4 us  [send(): lax.ppermute(value, 'tensor' if kind == 'x' else 'dp', ring(kind, step))]
    ppermute x39 -> x33, starting transfers between devices: 71.3 us -> 53.8 us  [send(): lax.ppermute(value, 'tensor' if kind == 'x' else 'dp', ring(kind, step))]
    all_to_all x1, starting transfers between devices: 3.53 us -> 12.5 us  [body(): both = lax.all_to_all(pack(right), 'dp', 0, 0, tiled=True)]
    unnamed x30 -> x16, local copies, waits for them, and re-layouts: 13.4 us -> 7.51 us
    pallas_call x3 -> x4, Pallas kernels: 18.2 us -> 21.7 us  [the longest x2 12.6 us: sketches(): call(sketch_kernel, [array(count, 2 * R), array(16, 128)], vmem=60 * 1024...]
  transfers between devices with their start and end apart: 48 -> 42, of which waited for: 29 -> 22; matrix products, arithmetic and copies ran while one was open for 2% -> 2% of each run, Pallas kernels for 11% -> 12%
where the time goes in v2:
time: 302 us; the launch traced here: 297 us
  starting transfers between devices  83 us (27%)
  waiting for transfers between devices  71.2 us (24%)
  Pallas kernels  65.5 us (22%)
  blocking collectives  46.6 us (15%)
  between operations  14.1 us (5%)
  local copies, waits for them, and re-layouts  11.2 us (4%)
  other arithmetic  5.32 us (2%)
    ppermute x33, waiting for transfers between devices, send(): lax.ppermute(value, 'tensor' if kind == 'x' else 'dp', ring(kind, step))  62.4 us
    ppermute x33, starting transfers between devices, send(): lax.ppermute(value, 'tensor' if kind == 'x' else 'dp', ring(kind, step))  53.8 us
    all_to_all x2, blocking collectives, exchange_x(): lax.all_to_all(value, 'tensor', 0, 0, axis_index_groups=groups, tiled=True)  46.6 us
    pallas_call x1, Pallas kernels, factors(): call(functools.partial(factor_kernel, counts), [array(R, R), array(R, R),...  14.1 us
    pallas_call x2, Pallas kernels, sketches(): call(sketch_kernel, [array(count, 2 * R), array(16, 128)], vmem=60 * 1024...  12.6 us
    pallas_call x1, Pallas kernels, ranges(): call(functools.partial(ranges_kernel, tokens_all), [array(R // 2, total)]...  12.5 us
    all_to_all x1, starting transfers between devices, body(): both = lax.all_to_all(pack(right), 'dp', 0, 0, tiled=True)  12.5 us
    ppermute x5, starting transfers between devices, swap_cores(): return lax.ppermute(value, 'tensor', [(i, i ^ 1) for i in range(8)])  11.1 us
  transfers between devices with their start and end apart: 42, of which 22 were waited for; matrix products, arithmetic and copies ran while one was open for 2% of the time, Pallas kernels for 12%

profile of v2, /device:TPU:1, one launch (start us, length us, event | category | flops | bytes accessed | tf_op | source)
XLA Modules:
  0.0 296.9 jit_solution(11187289063819529992)
XLA Ops:
  6.5 6.3 %sketches.3 = (f32[768,512]{1,0:T(8,128)}, f32[16,128]{1,0:T(8,128)}) custom-call(s32[1]{0:T(128)} %bitcast.2.core, bf16[1536,3072]{1,0:T(8,128)(2,1)} %grads.5, bf16[1536,768]{1,0:T(8,128)(2,1)} %acts.5, bf16[3072,256]{1,0:T(8,128)(2,1)} %sketch_out.3, bf16[768,256]{1,0:T(8,128)(2,1)} %sketch_in.3), custom_call_target="tpu_custom_call" | custom-call | tf_op jit(solution)/shard_map/sketches/pallas_call | solution.py:178
  12.8 1.4 collective-permute-start
  14.3 6.3 %sketches.2 = (f32[768,512]{1,0:T(8,128)}, f32[16,128]{1,0:T(8,128)}) custom-call(s32[1]{0:T(128)} %bitcast.1.core, bf16[1536,3072]{1,0:T(8,128)(2,1)} %grads.5, bf16[1536,768]{1,0:T(8,128)(2,1)} %acts.5, bf16[3072,256]{1,0:T(8,128)(2,1)} %sketch_out.3, bf16[768,256]{1,0:T(8,128)(2,1)} %sketch_in.3), custom_call_target="tpu_custom_call" | custom-call | tf_op jit(solution)/shard_map/sketches/pallas_call | solution.py:178
  20.5 1.8 add.325
  22.3 24.4 %all_to_all.28 = f32[4,192,512]{2,1,0:T(8,128)S(1)} all-to-all(f32[4,192,512]{2,1,0:T(8,128)S(1)} %bitcast.12), channel_id=1, replica_groups={{0,2,4,6},{1,3,5,7},{8,10,12,14},{9,11,13,15},{16,18,20,22},{17,19,21,2..., dimensions={0} | all-to-all | bytes 3145728 | tf_op jit(solution)/shard_map/all_to_all | solution.py:91
  47.1 22.2 %all_to_all.29 = f32[4,192,512]{2,1,0:T(8,128)S(1)} all-to-all(f32[4,192,512]{2,1,0:T(8,128)S(1)} %tile.2), channel_id=1, replica_groups={{0,2,4,6},{1,3,5,7},{8,10,12,14},{9,11,13,15},{16,18,20,22},{17,19,21,2..., dimensions={0} | all-to-all | bytes 3145728 | tf_op jit(solution)/shard_map/all_to_all | solution.py:91
  69.3 2.1 collective-permute-start.1
  71.4 3.0 collective-permute-done.1.other
  74.4 12.5 %ranges.1 = (f32[128,3968]{1,0:T(8,128)S(1)}, f32[128,3968]{1,0:T(8,128)}) custom-call(s32[2]{0:T(128)S(1)} %pad_add_fusion.places, f32[768,512]{1,0:T(8,128)S(1)} %bitcast.10, f32[768,512]{1,0:T(8,128)S(1)} %collective-permute-done.1.other, bf16[1536,3072]{1,0:T(8,128)(2,1)} %grads.5, bf16[1536,768]{1,0:T(8,128)(2,1)} %acts.5, f32[16,128]{1,0:T(8,128)S(1)} %copy-done.5, ...), custom_call_target="tpu_custom_call" | custom-call | tf_op jit(solution)/shard_map/ranges/pallas_call | solution.py:260
  86.9 1.3 copy-done.3
  88.2 1.2 constant_dynamic-slice_fusion.27
  89.4 2.9 collective-permute-start.2
  92.3 0.8 collective-permute-start.4
  93.9 3.7 %collective-permute-start.8 = (f32[32,3968]{1,0:T(8,128)S(1)}, f32[32,3968]{1,0:T(8,128)S(1)}, u32[]{:S(2)}, u32[]{:S(2)}) collective-permute-start(f32[32,3968]{1,0:T(8,128)S(1)} %get-tuple-element.27), channel_id=1, source_target_pairs={{0,64},{8,72},{16,80},{24,88},{32,96},{40,104},{48,112},{56,120},{... | collective-permute-start | bytes 1523720 | tf_op jit(solution)/shard_map/ppermute | solution.py:29
  98.0 5.9 %collective-permute-done.2 = f32[32,3968]{1,0:T(8,128)S(1)} collective-permute-done((f32[32,3968]{1,0:T(8,128)}, f32[32,3968]{1,0:T(8,128)S(1)}, u32[]{:S(2)}, u32[]{:S(2)}) %collective-permute-start.2) | collective-permute-done | bytes 507936 | tf_op jit(solution)/shard_map/ppermute | solution.py:29
  104.0 1.7 collective-permute-start.9
  105.6 9.6 %collective-permute-done.4 = f32[32,3968]{1,0:T(8,128)S(1)} collective-permute-done((f32[32,3968]{1,0:T(8,128)}, f32[32,3968]{1,0:T(8,128)S(1)}, u32[]{:S(2)}, u32[]{:S(2)}) %collective-permute-start.4) | collective-permute-done | bytes 507936 | tf_op jit(solution)/shard_map/ppermute | solution.py:29
  115.5 1.1 add_add_fusion.1
  116.7 3.7 %collective-permute-start.5 = (f32[8,3968]{1,0:T(8,128)S(1)}, f32[8,3968]{1,0:T(8,128)S(1)}, u32[]{:S(2)}, u32[]{:S(2)}) collective-permute-start(f32[8,3968]{1,0:T(8,128)S(1)} %get-tuple-element.44), channel_id=1, source_target_pairs={{0,64},{8,72},{16,80},{24,88},{32,96},{40,104},{48,112},{56,120},{... | collective-permute-start | bytes 380936 | tf_op jit(solution)/shard_map/ppermute | solution.py:29
  120.8 1.0 collective-permute-start.6
  122.0 3.0 %collective-permute-start.11 = (f32[8,3968]{1,0:T(8,128)S(1)}, f32[8,3968]{1,0:T(8,128)S(1)}, u32[]{:S(2)}, u32[]{:S(2)}) collective-permute-start(f32[8,3968]{1,0:T(8,128)S(1)} %get-tuple-element.41), channel_id=1, source_target_pairs={{0,16},{8,24},{16,0},{24,8},{32,48},{40,56},{48,32},{56,40},{64,80... | collective-permute-start | bytes 380936 | tf_op jit(solution)/shard_map/ppermute | solution.py:29
  126.6 0.8 collective-permute-done.11
  127.3 2.9 collective-permute-done.13
  130.2 1.1 collective-permute-done.12
  132.2 5.5 %collective-permute-start.14 = (f32[48,256]{1,0:T(8,128)S(1)}, f32[48,256]{1,0:T(8,128)S(1)}, u32[]{:S(2)}, u32[]{:S(2)}) collective-permute-start(f32[48,256]{1,0:T(8,128)S(1)} %pad_maximum_fusion.4), channel_id=1, source_target_pairs={{0,0},{1,16},{2,32},{3,48},{4,64},{5,80},{6,96},{7,112},{8,2},{9,1... | collective-permute-start | bytes 147464 | tf_op jit(solution)/shard_map/ppermute | solution.py:548
  137.8 1.3 collective-permute-done.14
  139.1 4.8 %collective-permute-start.17 = (f32[48,256]{1,0:T(8,128)S(1)}, f32[48,256]{1,0:T(8,128)S(1)}, u32[]{:S(2)}, u32[]{:S(2)}) collective-permute-start(f32[48,256]{1,0:T(8,128)S(1)} %collective-permute-done.14), channel_id=1, source_target_pairs={{0,6},{1,7},{2,0},{3,1},{4,2},{5,3},{6,4},{7,5},{8,14},{9,15},{10,... | collective-permute-start | bytes 147464 | tf_op jit(solution)/shard_map/ppermute | solution.py:29
  144.6 4.1 %collective-permute-done.15 = f32[48,256]{1,0:T(8,128)S(1)} collective-permute-done((f32[48,256]{1,0:T(8,128)S(1)}, f32[48,256]{1,0:T(8,128)S(1)}, u32[]{:S(2)}, u32[]{:S(2)}) %collective-permute-start.15) | collective-permute-done | bytes 49184 | tf_op jit(solution)/shard_map/ppermute | solution.py:29
  148.7 3.3 %collective-permute-start.18 = (f32[192,256]{1,0:T(8,128)S(1)}, f32[192,256]{1,0:T(8,128)S(1)}, u32[]{:S(2)}, u32[]{:S(2)}) collective-permute-start(f32[192,256]{1,0:T(8,128)S(1)} %constant_dynamic-update-slice_fusion.4), channel_id=1, source_target_pairs={{0,1},{1,0},{2,3},{3,2},{4,5},{5,4},{6,7},{7,6},{8,9},{9,8},{10,11... | collective-permute-start | bytes 589832 | tf_op jit(solution)/shard_map/ppermute | solution.py:33
  152.0 1.1 collective-permute-done.18
  153.2 5.8 %left_products.1 = (f32[128,3072]{1,0:T(8,128)S(1)}, f32[128,3072]{1,0:T(8,128)S(1)}) custom-call(f32[384,256]{1,0:T(8,128)S(1)} %pad_maximum_fusion.2.rows_act, f32[384,3072]{1,0:T(8,128)} %weight.3), custom_call_target="tpu_custom_call" | custom-call | tf_op jit(solution)/shard_map/left_products/pallas_call | solution.py:282
  159.2 4.6 %collective-permute-start.21 = (f32[32,3072]{1,0:T(8,128)S(1)}, f32[32,3072]{1,0:T(8,128)S(1)}, u32[]{:S(2)}, u32[]{:S(2)}) collective-permute-start(f32[32,3072]{1,0:T(8,128)S(1)} %get-tuple-element.36), channel_id=1, source_target_pairs={{0,24},{8,0},{16,8},{24,16},{32,56},{40,32},{48,40},{56,48},{64,88... | collective-permute-start | bytes 1179656 | tf_op jit(solution)/shard_map/ppermute | solution.py:29
  163.9 1.3 collective-permute-start.25
  165.2 0.8 collective-permute-start.27
  166.0 10.4 %collective-permute-done.19 = f32[32,3072]{1,0:T(8,128)S(1)} collective-permute-done((f32[32,3072]{1,0:T(8,128)S(1)}, f32[32,3072]{1,0:T(8,128)S(1)}, u32[]{:S(2)}, u32[]{:S(2)}) %collective-permute-start.19) | collective-permute-done | bytes 393248 | tf_op jit(solution)/shard_map/ppermute | solution.py:29
  176.4 1.6 collective-permute-start.26
  178.0 13.5 %collective-permute-done.21 = f32[32,3072]{1,0:T(8,128)S(1)} collective-permute-done((f32[32,3072]{1,0:T(8,128)S(1)}, f32[32,3072]{1,0:T(8,128)S(1)}, u32[]{:S(2)}, u32[]{:S(2)}) %collective-permute-start.21) | collective-permute-done | bytes 393248 | tf_op jit(solution)/shard_map/ppermute | solution.py:29
  191.7 1.9 collective-permute-start.22
  193.6 1.8 collective-permute-start.24
  195.8 0.8 collective-permute-done.27
  196.7 4.6 %collective-permute-start.28 = (f32[8,3072]{1,0:T(8,128)S(1)}, f32[8,3072]{1,0:T(8,128)S(1)}, u32[]{:S(2)}, u32[]{:S(2)}) collective-permute-start(f32[8,3072]{1,0:T(8,128)S(1)} %get-tuple-element.53), channel_id=1, source_target_pairs={{0,16},{8,24},{16,0},{24,8},{32,48},{40,56},{48,32},{56,40},{64,80... | collective-permute-start | bytes 294920 | tf_op jit(solution)/shard_map/ppermute | solution.py:29
  201.9 0.9 collective-permute-start.29
  203.4 1.5 collective-permute-done.30
  204.9 2.7 collective-permute-done.29
  208.4 2.1 copy-done
  210.5 7.3 %right_products.1 = f32[896,256]{1,0:T(8,128)S(1)} custom-call(f32[256,3968]{1,0:T(8,128)S(1)} %copy-done, f32[256,3968]{1,0:T(8,128)S(1)} %copy-done, f32[256,3968]{1,0:T(8,128)S(1)} %copy-done, f32[256,3968]{1,0:T(8,128)S(1)} %copy-done, f32[256,3968]{1,0:T(8,128)S(1)} %copy-done, f32[256,3968]{1,0:T(8,128)S(1)} %copy-done, f32[256,3968]{1,0:T(8,128)S(1)} %copy-done, ...), custom_call_target="tpu_custom_call" | custom-call | tf_op jit(solution)/shard_map/right_products/pallas_call | solution.py:320
  217.8 2.7 collective-permute-start.31
  220.6 1.4 collective-permute-done.31
  222.1 4.5 %collective-permute-start.32 = (f32[112,256]{1,0:T(8,128)S(1)}, f32[112,256]{1,0:T(8,128)S(1)}, u32[]{:S(2)}, u32[]{:S(2)}) collective-permute-start(f32[112,256]{1,0:T(8,128)S(1)} %get-tuple-element.47), channel_id=1, source_target_pairs={{0,4},{1,5},{2,6},{3,7},{4,0},{5,1},{6,2},{7,3},{8,12},{9,13},{10,... | collective-permute-start | bytes 344072 | tf_op jit(solution)/shard_map/ppermute | solution.py:29
  226.6 1.5 collective-permute-start.33
  228.1 0.9 slice_bitcast_fusion
  229.7 2.1 copy-done.1
  231.9 1.9 both_products.1
  234.0 2.4 collective-permute-start.36
  236.4 1.5 collective-permute-start.37
  237.9 2.7 collective-permute-done.35
  240.6 4.4 %collective-permute-done.36 = f32[200,256]{1,0:T(8,128)S(1)} collective-permute-done((f32[200,256]{1,0:T(8,128)S(1)}, f32[200,256]{1,0:T(8,128)S(1)}, u32[]{:S(2)}, u32[]{:S(2)}) %collective-permute-start.36) | collective-permute-done | bytes 204832 | tf_op jit(solution)/shard_map/ppermute | solution.py:29
  245.1 1.1 collective-permute-done.37
  246.2 1.6 collective-permute-start.38
  247.8 2.0 collective-permute-done.38
  250.7 12.5 %all-to-all-start.2 = ((f32[16,16,256]{2,1,0:T(8,128)}), f32[16,16,256]{2,1,0:T(8,128)S(1)}, u32[]{:S(2)}, u32[]{:S(2)}) async-start(f32[16,16,256]{2,1,0:T(8,128)} %bitcast.6), calls=%async_computation.2 | async-start | bytes 524288 | tf_op jit(solution)/shard_map/all_to_all | solution.py:559
  263.2 14.1 %factors.1 = (f32[256,256]{1,0:T(8,128)S(1)}, f32[256,256]{1,0:T(8,128)S(1)}, f32[8,128]{1,0:T(8,128)S(1)}) custom-call(f32[1600,256]{1,0:T(8,128)S(1)} %pad_maximum_fusion.right), custom_call_target="tpu_custom_call" | custom-call | tf_op jit(solution)/shard_map/factors/pallas_call | solution.py:464
  277.4 1.9 copy-done.2
  279.3 10.5 %last_update.1 = f32[384,3072]{1,0:T(8,128)} custom-call(f32[256,3072]{1,0:T(8,128)S(1)} %copy-done.2, f32[384,3072]{1,0:T(8,128)} %weight.3, f32[256,3968]{1,0:T(8,128)} %all-gather.5.cloned.1.call-done.whole.refs_0_.refs_1_.refs_2_.refs_3_.refs_4_.refs_5_.range_grad, f32[1600,256]{1,0:T(8,128)S(1)} %pad_maximum_fusion.right, f32[256,256]{1,0:T(8,128)S(1)} %bitcast.11, ...), custom_call_target="tpu_custom_call" | custom-call | tf_op jit(solution)/shard_map/last_update/pallas_call | solution.py:500
  (94 shorter events, 10.8 us)
Async XLA Ops:
  6.5 201.8 %all-gather.5.cloned.1.call-start = ((), (), s32[]{:S(2)}) async-start(), calls=%async_computation.4 | async-start | bytes 4317184 | tf_op jit(solution)/shard_map/all_gather | solution.py:539
  12.8 7.7 %collective-permute-start = (f32[768,512]{1,0:T(8,128)}, f32[768,512]{1,0:T(8,128)S(1)}, u32[]{:S(2)}, u32[]{:S(2)}) collective-permute-start(f32[768,512]{1,0:T(8,128)} %get-tuple-element.17), channel_id=1, source_target_pairs={{0,1},{1,0},{2,3},{3,2},{4,5},{5,4},{6,7},{7,6},{8,9},{9,8},{10,11... | collective-permute-start | bytes 4718600 | tf_op jit(solution)/shard_map/ppermute | solution.py:33
  47.1 27.3 %copy-start.5 = (f32[16,128]{1,0:T(8,128)S(1)}, f32[16,128]{1,0:T(8,128)}, u32[]{:S(2)}) copy-start(f32[16,128]{1,0:T(8,128)} %get-tuple-element.18.sq_one) | copy-start | bytes 24580
  47.1 27.3 %copy-start.6 = (f32[16,128]{1,0:T(8,128)S(1)}, f32[16,128]{1,0:T(8,128)}, u32[]{:S(2)}) copy-start(f32[16,128]{1,0:T(8,128)} %get-tuple-element.19.sq_two) | copy-start | bytes 24580
  69.3 5.1 %collective-permute-start.1 = (f32[768,512]{1,0:T(8,128)S(1)}, f32[768,512]{1,0:T(8,128)S(1)}, u32[]{:S(2)}, u32[]{:S(2)}) collective-permute-start(f32[768,512]{1,0:T(8,128)S(1)} %bitcast.9), channel_id=1, source_target_pairs={{0,1},{1,0},{2,3},{3,2},{4,5},{5,4},{6,7},{7,6},{8,9},{9,8},{10,11... | collective-permute-start | bytes 4718600 | tf_op jit(solution)/shard_map/ppermute | solution.py:33
  86.9 1.3 copy-start.3
  86.9 6.9 %copy-start.7 = (f32[128,3968]{1,0:T(8,128)S(1)}, f32[128,3968]{1,0:T(8,128)}, u32[]{:S(2)}) copy-start(f32[128,3968]{1,0:T(8,128)} %get-tuple-element.21) | copy-start | bytes 6094852
  89.4 14.5 %collective-permute-start.2 = (f32[32,3968]{1,0:T(8,128)}, f32[32,3968]{1,0:T(8,128)S(1)}, u32[]{:S(2)}, u32[]{:S(2)}) collective-permute-start(f32[32,3968]{1,0:T(8,128)} %get-tuple-element.30), channel_id=1, source_target_pairs={{0,16},{8,24},{16,0},{24,8},{32,48},{40,56},{48,32},{56,40},{64,80... | collective-permute-start | bytes 1523720 | tf_op jit(solution)/shard_map/ppermute | solution.py:29
  92.3 22.9 %collective-permute-start.4 = (f32[32,3968]{1,0:T(8,128)}, f32[32,3968]{1,0:T(8,128)S(1)}, u32[]{:S(2)}, u32[]{:S(2)}) collective-permute-start(f32[32,3968]{1,0:T(8,128)} %get-tuple-element.31), channel_id=1, source_target_pairs={{0,24},{8,0},{16,8},{24,16},{32,56},{40,32},{48,40},{56,48},{64,88... | collective-permute-start | bytes 1523720 | tf_op jit(solution)/shard_map/ppermute | solution.py:29
  93.1 22.4 %collective-permute-start.3 = (f32[32,3968]{1,0:T(8,128)}, f32[32,3968]{1,0:T(8,128)S(1)}, u32[]{:S(2)}, u32[]{:S(2)}) collective-permute-start(f32[32,3968]{1,0:T(8,128)} %get-tuple-element.32), channel_id=1, source_target_pairs={{0,8},{8,16},{16,24},{24,0},{32,40},{40,48},{48,56},{56,32},{64,72... | collective-permute-start | bytes 1523720 | tf_op jit(solution)/shard_map/ppermute | solution.py:29
  93.9 26.9 %collective-permute-start.8 = (f32[32,3968]{1,0:T(8,128)S(1)}, f32[32,3968]{1,0:T(8,128)S(1)}, u32[]{:S(2)}, u32[]{:S(2)}) collective-permute-start(f32[32,3968]{1,0:T(8,128)S(1)} %get-tuple-element.27), channel_id=1, source_target_pairs={{0,64},{8,72},{16,80},{24,88},{32,96},{40,104},{48,112},{56,120},{... | collective-permute-start | bytes 1523720 | tf_op jit(solution)/shard_map/ppermute | solution.py:29
  97.6 24.2 %collective-permute-start.10 = (f32[32,3968]{1,0:T(8,128)S(1)}, f32[32,3968]{1,0:T(8,128)S(1)}, u32[]{:S(2)}, u32[]{:S(2)}) collective-permute-start(f32[32,3968]{1,0:T(8,128)S(1)} %get-tuple-element.28), channel_id=1, source_target_pairs={{0,96},{8,104},{16,112},{24,120},{32,0},{40,8},{48,16},{56,24},{64... | collective-permute-start | bytes 1523720 | tf_op jit(solution)/shard_map/ppermute | solution.py:29
  104.0 17.9 %collective-permute-start.9 = (f32[32,3968]{1,0:T(8,128)S(1)}, f32[32,3968]{1,0:T(8,128)S(1)}, u32[]{:S(2)}, u32[]{:S(2)}) collective-permute-start(f32[32,3968]{1,0:T(8,128)S(1)} %get-tuple-element.29), channel_id=1, source_target_pairs={{0,32},{8,40},{16,48},{24,56},{32,64},{40,72},{48,80},{56,88},{64,... | collective-permute-start | bytes 1523720 | tf_op jit(solution)/shard_map/ppermute | solution.py:29
  116.7 9.1 %collective-permute-start.5 = (f32[8,3968]{1,0:T(8,128)S(1)}, f32[8,3968]{1,0:T(8,128)S(1)}, u32[]{:S(2)}, u32[]{:S(2)}) collective-permute-start(f32[8,3968]{1,0:T(8,128)S(1)} %get-tuple-element.44), channel_id=1, source_target_pairs={{0,64},{8,72},{16,80},{24,88},{32,96},{40,104},{48,112},{56,120},{... | collective-permute-start | bytes 380936 | tf_op jit(solution)/shard_map/ppermute | solution.py:29
  120.4 6.1 %collective-permute-start.7 = (f32[8,3968]{1,0:T(8,128)S(1)}, f32[8,3968]{1,0:T(8,128)S(1)}, u32[]{:S(2)}, u32[]{:S(2)}) collective-permute-start(f32[8,3968]{1,0:T(8,128)S(1)} %get-tuple-element.45), channel_id=1, source_target_pairs={{0,96},{8,104},{16,112},{24,120},{32,0},{40,8},{48,16},{56,24},{64... | collective-permute-start | bytes 380936 | tf_op jit(solution)/shard_map/ppermute | solution.py:29
  120.8 5.7 %collective-permute-start.6 = (f32[8,3968]{1,0:T(8,128)S(1)}, f32[8,3968]{1,0:T(8,128)S(1)}, u32[]{:S(2)}, u32[]{:S(2)}) collective-permute-start(f32[8,3968]{1,0:T(8,128)S(1)} %get-tuple-element.46), channel_id=1, source_target_pairs={{0,32},{8,40},{16,48},{24,56},{32,64},{40,72},{48,80},{56,88},{64,... | collective-permute-start | bytes 380936 | tf_op jit(solution)/shard_map/ppermute | solution.py:29
  122.0 5.4 %collective-permute-start.11 = (f32[8,3968]{1,0:T(8,128)S(1)}, f32[8,3968]{1,0:T(8,128)S(1)}, u32[]{:S(2)}, u32[]{:S(2)}) collective-permute-start(f32[8,3968]{1,0:T(8,128)S(1)} %get-tuple-element.41), channel_id=1, source_target_pairs={{0,16},{8,24},{16,0},{24,8},{32,48},{40,56},{48,32},{56,40},{64,80... | collective-permute-start | bytes 380936 | tf_op jit(solution)/shard_map/ppermute | solution.py:29
  125.0 5.2 %collective-permute-start.13 = (f32[8,3968]{1,0:T(8,128)S(1)}, f32[8,3968]{1,0:T(8,128)S(1)}, u32[]{:S(2)}, u32[]{:S(2)}) collective-permute-start(f32[8,3968]{1,0:T(8,128)S(1)} %get-tuple-element.42), channel_id=1, source_target_pairs={{0,24},{8,0},{16,8},{24,16},{32,56},{40,32},{48,40},{56,48},{64,88... | collective-permute-start | bytes 380936 | tf_op jit(solution)/shard_map/ppermute | solution.py:29
  125.8 5.6 %collective-permute-start.12 = (f32[8,3968]{1,0:T(8,128)S(1)}, f32[8,3968]{1,0:T(8,128)S(1)}, u32[]{:S(2)}, u32[]{:S(2)}) collective-permute-start(f32[8,3968]{1,0:T(8,128)S(1)} %get-tuple-element.43), channel_id=1, source_target_pairs={{0,8},{8,16},{16,24},{24,0},{32,40},{40,48},{48,56},{56,32},{64,72... | collective-permute-start | bytes 380936 | tf_op jit(solution)/shard_map/ppermute | solution.py:29
  132.1 145.3 %all-gather.3.cloned.1.call-start = ((), (), s32[]{:S(2)}) async-start(), calls=%async_computation.3 | async-start | bytes 3342336 | tf_op jit(solution)/shard_map/all_gather | solution.py:551
  132.2 6.9 %collective-permute-start.14 = (f32[48,256]{1,0:T(8,128)S(1)}, f32[48,256]{1,0:T(8,128)S(1)}, u32[]{:S(2)}, u32[]{:S(2)}) collective-permute-start(f32[48,256]{1,0:T(8,128)S(1)} %pad_maximum_fusion.4), channel_id=1, source_target_pairs={{0,0},{1,16},{2,32},{3,48},{4,64},{5,80},{6,96},{7,112},{8,2},{9,1... | collective-permute-start | bytes 147464 | tf_op jit(solution)/shard_map/ppermute | solution.py:548
  139.1 9.6 %collective-permute-start.17 = (f32[48,256]{1,0:T(8,128)S(1)}, f32[48,256]{1,0:T(8,128)S(1)}, u32[]{:S(2)}, u32[]{:S(2)}) collective-permute-start(f32[48,256]{1,0:T(8,128)S(1)} %collective-permute-done.14), channel_id=1, source_target_pairs={{0,6},{1,7},{2,0},{3,1},{4,2},{5,3},{6,4},{7,5},{8,14},{9,15},{10,... | collective-permute-start | bytes 147464 | tf_op jit(solution)/shard_map/ppermute | solution.py:29
  143.9 4.8 %collective-permute-start.16 = (f32[48,256]{1,0:T(8,128)S(1)}, f32[48,256]{1,0:T(8,128)S(1)}, u32[]{:S(2)}, u32[]{:S(2)}) collective-permute-start(f32[48,256]{1,0:T(8,128)S(1)} %collective-permute-done.14), channel_id=1, source_target_pairs={{0,4},{1,5},{2,6},{3,7},{4,0},{5,1},{6,2},{7,3},{8,12},{9,13},{10,... | collective-permute-start | bytes 147464 | tf_op jit(solution)/shard_map/ppermute | solution.py:29
  143.9 4.8 %collective-permute-start.15 = (f32[48,256]{1,0:T(8,128)S(1)}, f32[48,256]{1,0:T(8,128)S(1)}, u32[]{:S(2)}, u32[]{:S(2)}) collective-permute-start(f32[48,256]{1,0:T(8,128)S(1)} %collective-permute-done.14), channel_id=1, source_target_pairs={{0,2},{1,3},{2,4},{3,5},{4,6},{5,7},{6,0},{7,1},{8,10},{9,11},{10,... | collective-permute-start | bytes 147464 | tf_op jit(solution)/shard_map/ppermute | solution.py:29
  148.7 4.4 %collective-permute-start.18 = (f32[192,256]{1,0:T(8,128)S(1)}, f32[192,256]{1,0:T(8,128)S(1)}, u32[]{:S(2)}, u32[]{:S(2)}) collective-permute-start(f32[192,256]{1,0:T(8,128)S(1)} %constant_dynamic-update-slice_fusion.4), channel_id=1, source_target_pairs={{0,1},{1,0},{2,3},{3,2},{4,5},{5,4},{6,7},{7,6},{8,9},{9,8},{10,11... | collective-permute-start | bytes 589832 | tf_op jit(solution)/shard_map/ppermute | solution.py:33
  159.1 17.3 %collective-permute-start.19 = (f32[32,3072]{1,0:T(8,128)S(1)}, f32[32,3072]{1,0:T(8,128)S(1)}, u32[]{:S(2)}, u32[]{:S(2)}) collective-permute-start(f32[32,3072]{1,0:T(8,128)S(1)} %get-tuple-element.35), channel_id=1, source_target_pairs={{0,16},{8,24},{16,0},{24,8},{32,48},{40,56},{48,32},{56,40},{64,80... | collective-permute-start | bytes 1179656 | tf_op jit(solution)/shard_map/ppermute | solution.py:29
  159.2 32.4 %collective-permute-start.21 = (f32[32,3072]{1,0:T(8,128)S(1)}, f32[32,3072]{1,0:T(8,128)S(1)}, u32[]{:S(2)}, u32[]{:S(2)}) collective-permute-start(f32[32,3072]{1,0:T(8,128)S(1)} %get-tuple-element.36), channel_id=1, source_target_pairs={{0,24},{8,0},{16,8},{24,16},{32,56},{40,32},{48,40},{56,48},{64,88... | collective-permute-start | bytes 1179656 | tf_op jit(solution)/shard_map/ppermute | solution.py:29
  163.8 27.8 %collective-permute-start.20 = (f32[32,3072]{1,0:T(8,128)S(1)}, f32[32,3072]{1,0:T(8,128)S(1)}, u32[]{:S(2)}, u32[]{:S(2)}) collective-permute-start(f32[32,3072]{1,0:T(8,128)S(1)} %get-tuple-element.37), channel_id=1, source_target_pairs={{0,8},{8,16},{16,24},{24,0},{32,40},{40,48},{48,56},{56,32},{64,72... | collective-permute-start | bytes 1179656 | tf_op jit(solution)/shard_map/ppermute | solution.py:29
  163.9 31.5 %collective-permute-start.25 = (f32[32,3072]{1,0:T(8,128)S(1)}, f32[32,3072]{1,0:T(8,128)S(1)}, u32[]{:S(2)}, u32[]{:S(2)}) collective-permute-start(f32[32,3072]{1,0:T(8,128)S(1)} %get-tuple-element.38), channel_id=1, source_target_pairs={{0,64},{8,72},{16,80},{24,88},{32,96},{40,104},{48,112},{56,120},{... | collective-permute-start | bytes 1179656 | tf_op jit(solution)/shard_map/ppermute | solution.py:29
  165.2 31.4 %collective-permute-start.27 = (f32[32,3072]{1,0:T(8,128)S(1)}, f32[32,3072]{1,0:T(8,128)S(1)}, u32[]{:S(2)}, u32[]{:S(2)}) collective-permute-start(f32[32,3072]{1,0:T(8,128)S(1)} %get-tuple-element.39), channel_id=1, source_target_pairs={{0,96},{8,104},{16,112},{24,120},{32,0},{40,8},{48,16},{56,24},{64... | collective-permute-start | bytes 1179656 | tf_op jit(solution)/shard_map/ppermute | solution.py:29
  176.4 20.2 %collective-permute-start.26 = (f32[32,3072]{1,0:T(8,128)S(1)}, f32[32,3072]{1,0:T(8,128)S(1)}, u32[]{:S(2)}, u32[]{:S(2)}) collective-permute-start(f32[32,3072]{1,0:T(8,128)S(1)} %get-tuple-element.40), channel_id=1, source_target_pairs={{0,32},{8,40},{16,48},{24,56},{32,64},{40,72},{48,80},{56,88},{64,... | collective-permute-start | bytes 1179656 | tf_op jit(solution)/shard_map/ppermute | solution.py:29
  191.7 10.2 %collective-permute-start.22 = (f32[8,3072]{1,0:T(8,128)S(1)}, f32[8,3072]{1,0:T(8,128)S(1)}, u32[]{:S(2)}, u32[]{:S(2)}) collective-permute-start(f32[8,3072]{1,0:T(8,128)S(1)} %get-tuple-element.50), channel_id=1, source_target_pairs={{0,64},{8,72},{16,80},{24,88},{32,96},{40,104},{48,112},{56,120},{... | collective-permute-start | bytes 294920 | tf_op jit(solution)/shard_map/ppermute | solution.py:29
  193.6 9.3 %collective-permute-start.24 = (f32[8,3072]{1,0:T(8,128)S(1)}, f32[8,3072]{1,0:T(8,128)S(1)}, u32[]{:S(2)}, u32[]{:S(2)}) collective-permute-start(f32[8,3072]{1,0:T(8,128)S(1)} %get-tuple-element.51), channel_id=1, source_target_pairs={{0,96},{8,104},{16,112},{24,120},{32,0},{40,8},{48,16},{56,24},{64... | collective-permute-start | bytes 294920 | tf_op jit(solution)/shard_map/ppermute | solution.py:29
  195.3 7.5 %collective-permute-start.23 = (f32[8,3072]{1,0:T(8,128)S(1)}, f32[8,3072]{1,0:T(8,128)S(1)}, u32[]{:S(2)}, u32[]{:S(2)}) collective-permute-start(f32[8,3072]{1,0:T(8,128)S(1)} %get-tuple-element.52), channel_id=1, source_target_pairs={{0,32},{8,40},{16,48},{24,56},{32,64},{40,72},{48,80},{56,88},{64,... | collective-permute-start | bytes 294920 | tf_op jit(solution)/shard_map/ppermute | solution.py:29
  196.7 6.7 %collective-permute-start.28 = (f32[8,3072]{1,0:T(8,128)S(1)}, f32[8,3072]{1,0:T(8,128)S(1)}, u32[]{:S(2)}, u32[]{:S(2)}) collective-permute-start(f32[8,3072]{1,0:T(8,128)S(1)} %get-tuple-element.53), channel_id=1, source_target_pairs={{0,16},{8,24},{16,0},{24,8},{32,48},{40,56},{48,32},{56,40},{64,80... | collective-permute-start | bytes 294920 | tf_op jit(solution)/shard_map/ppermute | solution.py:29
  201.4 3.5 %collective-permute-start.30 = (f32[8,3072]{1,0:T(8,128)S(1)}, f32[8,3072]{1,0:T(8,128)S(1)}, u32[]{:S(2)}, u32[]{:S(2)}) collective-permute-start(f32[8,3072]{1,0:T(8,128)S(1)} %get-tuple-element.54), channel_id=1, source_target_pairs={{0,24},{8,0},{16,8},{24,16},{32,56},{40,32},{48,40},{56,48},{64,88... | collective-permute-start | bytes 294920 | tf_op jit(solution)/shard_map/ppermute | solution.py:29
  201.9 5.6 %collective-permute-start.29 = (f32[8,3072]{1,0:T(8,128)S(1)}, f32[8,3072]{1,0:T(8,128)S(1)}, u32[]{:S(2)}, u32[]{:S(2)}) collective-permute-start(f32[8,3072]{1,0:T(8,128)S(1)} %get-tuple-element.55), channel_id=1, source_target_pairs={{0,8},{8,16},{16,24},{24,0},{32,40},{40,48},{48,56},{56,32},{64,72... | collective-permute-start | bytes 294920 | tf_op jit(solution)/shard_map/ppermute | solution.py:29
  208.3 2.2 copy-start
  217.8 12.0 %copy-start.4 = (f32[16,3072]{1,0:T(8,128)S(1)}, f32[16,3072]{1,0:T(8,128)}, u32[]{:S(2)}) copy-start(f32[16,3072]{1,0:T(8,128)} %pad_maximum_fusion.3.left) | copy-start | bytes 589828
  217.8 4.2 %collective-permute-start.31 = (f32[448,256]{1,0:T(8,128)S(1)}, f32[448,256]{1,0:T(8,128)S(1)}, u32[]{:S(2)}, u32[]{:S(2)}) collective-permute-start(f32[448,256]{1,0:T(8,128)S(1)} %constant_dynamic-slice_fusion.3), channel_id=1, source_target_pairs={{0,1},{1,0},{2,3},{3,2},{4,5},{5,4},{6,7},{7,6},{8,9},{9,8},{10,11... | collective-permute-start | bytes 1376264 | tf_op jit(solution)/shard_map/ppermute | solution.py:33
  222.1 11.7 %collective-permute-start.32 = (f32[112,256]{1,0:T(8,128)S(1)}, f32[112,256]{1,0:T(8,128)S(1)}, u32[]{:S(2)}, u32[]{:S(2)}) collective-permute-start(f32[112,256]{1,0:T(8,128)S(1)} %get-tuple-element.47), channel_id=1, source_target_pairs={{0,4},{1,5},{2,6},{3,7},{4,0},{5,1},{6,2},{7,3},{8,12},{9,13},{10,... | collective-permute-start | bytes 344072 | tf_op jit(solution)/shard_map/ppermute | solution.py:29
  226.6 7.2 %collective-permute-start.34 = (f32[112,256]{1,0:T(8,128)S(1)}, f32[112,256]{1,0:T(8,128)S(1)}, u32[]{:S(2)}, u32[]{:S(2)}) collective-permute-start(f32[112,256]{1,0:T(8,128)S(1)} %get-tuple-element.48), channel_id=1, source_target_pairs={{0,6},{1,7},{2,0},{3,1},{4,2},{5,3},{6,4},{7,5},{8,14},{9,15},{10,... | collective-permute-start | bytes 344072 | tf_op jit(solution)/shard_map/ppermute | solution.py:29
  226.6 7.2 %collective-permute-start.33 = (f32[112,256]{1,0:T(8,128)S(1)}, f32[112,256]{1,0:T(8,128)S(1)}, u32[]{:S(2)}, u32[]{:S(2)}) collective-permute-start(f32[112,256]{1,0:T(8,128)S(1)} %get-tuple-element.49), channel_id=1, source_target_pairs={{0,2},{1,3},{2,4},{3,5},{4,6},{5,7},{6,0},{7,1},{8,10},{9,11},{10,... | collective-permute-start | bytes 344072 | tf_op jit(solution)/shard_map/ppermute | solution.py:29
  229.7 2.2 copy-start.1
  234.0 6.6 %collective-permute-start.35 = (f32[200,256]{1,0:T(8,128)S(1)}, f32[200,256]{1,0:T(8,128)S(1)}, u32[]{:S(2)}, u32[]{:S(2)}) collective-permute-start(f32[200,256]{1,0:T(8,128)S(1)} %get-tuple-element.61), channel_id=1, source_target_pairs={{0,2},{1,3},{2,4},{3,5},{4,6},{5,7},{6,0},{7,1},{8,10},{9,11},{10,... | collective-permute-start | bytes 614408 | tf_op jit(solution)/shard_map/ppermute | solution.py:29
  234.0 11.0 %collective-permute-start.36 = (f32[200,256]{1,0:T(8,128)S(1)}, f32[200,256]{1,0:T(8,128)S(1)}, u32[]{:S(2)}, u32[]{:S(2)}) collective-permute-start(f32[200,256]{1,0:T(8,128)S(1)} %get-tuple-element.61), channel_id=1, source_target_pairs={{0,4},{1,5},{2,6},{3,7},{4,0},{5,1},{6,2},{7,3},{8,12},{9,13},{10,... | collective-permute-start | bytes 614408 | tf_op jit(solution)/shard_map/ppermute | solution.py:29
  236.4 9.8 %collective-permute-start.37 = (f32[200,256]{1,0:T(8,128)S(1)}, f32[200,256]{1,0:T(8,128)S(1)}, u32[]{:S(2)}, u32[]{:S(2)}) collective-permute-start(f32[200,256]{1,0:T(8,128)S(1)} %get-tuple-element.61), channel_id=1, source_target_pairs={{0,6},{1,7},{2,0},{3,1},{4,2},{5,3},{6,4},{7,5},{8,14},{9,15},{10,... | collective-permute-start | bytes 614408 | tf_op jit(solution)/shard_map/ppermute | solution.py:29
  246.2 3.6 %collective-permute-start.38 = (f32[800,256]{1,0:T(8,128)S(1)}, f32[800,256]{1,0:T(8,128)S(1)}, u32[]{:S(2)}, u32[]{:S(2)}) collective-permute-start(f32[800,256]{1,0:T(8,128)S(1)} %constant_dynamic-update-slice_fusion), channel_id=1, source_target_pairs={{0,1},{1,0},{2,3},{3,2},{4,5},{5,4},{6,7},{7,6},{8,9},{9,8},{10,11... | collective-permute-start | bytes 2457608 | tf_op jit(solution)/shard_map/ppermute | solution.py:33
  250.7 26.7 %all-to-all-start.2 = ((f32[16,16,256]{2,1,0:T(8,128)}), f32[16,16,256]{2,1,0:T(8,128)S(1)}, u32[]{:S(2)}, u32[]{:S(2)}) async-start(f32[16,16,256]{2,1,0:T(8,128)} %bitcast.6), calls=%async_computation.2 | async-start | bytes 524288 | tf_op jit(solution)/shard_map/all_to_all | solution.py:559
  277.4 1.9 copy-start.2
Sparse Core Ops, SparseCore 0:
  132.2 67.0 all-gather.4
  208.4 47.7 all-gather.2
